TPU v7x, 32 devices: a whole 2x2x4 slice. The times are simulated.
32 devices in a mesh: seq: 8 (over y, x, core), head: 4 (over z).
Axes of the slice: x: 2, y: 2, z: 4, core: 2. Of those that a mesh axis runs over, the one named last changes fastest.
Arguments:
- stream: bfloat16 [8192, 1536], P('seq'), may hold values from -6 to 6
- prescale: float32 [1536], replicated, may hold values from 0.25 to 1.75
- gelumat: bfloat16 [1536, 2048], P(None, 'head'), may hold values from -0.15625 to 0.15625
- gelubias: float32 [2048], P('head'), may hold values from -3 to 3
- lrumat: bfloat16 [1536, 2048], P(None, 'head'), may hold values from -0.15625 to 0.15625
- lrubias: float32 [2048], P('head'), may hold values from -3 to 3
- convtaps: float32 [4, 2048], P(None, 'head'), may hold values from -3 to 3
- convbias: float32 [2048], P('head'), may hold values from -2 to 2
- recgates: bfloat16 [16, 128, 128], P('head'), may hold values from -0.5 to 0.5
- recbias: float32 [2048], P('head'), may hold values from -3 to 3
- inpgates: bfloat16 [16, 128, 128], P('head'), may hold values from -0.5 to 0.5
- inpbias: float32 [2048], P('head'), may hold values from -3 to 3
- lambdas: float32 [2048], P('head'), may hold values from 4 to 16
- outmat: bfloat16 [2048, 1536], P('head'), may hold values from -0.375 to 0.375
- midscale: float32 [1536], replicated, may hold values from 0.25 to 1.75
- gatemat: bfloat16 [1536, 4608], P(None, 'head'), may hold values from -0.15625 to 0.15625
- upmatrix: bfloat16 [1536, 4608], P(None, 'head'), may hold values from -0.15625 to 0.15625
- downmat: bfloat16 [4608, 1536], P('head'), may hold values from -0.1875 to 0.1875
- resets: int32 [8192], P('seq'), may hold values from 0 to 1, as said below
- cotangent: bfloat16 [8192, 1536], P('seq'), may hold values from -6 to 6
Outputs:
- block_output: bfloat16 [8192, 1536], P('seq')
- grad_stream: bfloat16 [8192, 1536], P('seq')
- grad_prescale: float32 [1536], P('seq')
- grad_gelumat: float32 [1536, 2048], P('seq', 'head')
- grad_gelubias: float32 [2048], P('head')
- grad_lrumat: float32 [1536, 2048], P('seq', 'head')
- grad_lrubias: float32 [2048], P('head')
- grad_convtaps: float32 [4, 2048], P(None, 'head')
- grad_convbias: float32 [2048], P('head')
- grad_recgates: float32 [16, 128, 128], P('head')
- grad_recbias: float32 [2048], P('head')
- grad_inpgates: float32 [16, 128, 128], P('head')
- grad_inpbias: float32 [2048], P('head')
- grad_lambdas: float32 [2048], P('head')
- grad_outmat: float32 [2048, 1536], P('head', 'seq')
- grad_midscale: float32 [1536], P('seq')
- grad_gatemat: float32 [1536, 4608], P('seq', 'head')
- grad_upmatrix: float32 [1536, 4608], P('seq', 'head')
- grad_downmat: float32 [4608, 1536], P('head', 'seq')
Inputs may be any that keep to these rules, and one draw needn't show every extreme that they name: `resets`: position 0 is a document start. One document starts within the first 512 tokens and ends within the last 512 tokens of the stream.
All inputs are finite; a program needn't handle non-finite values.
Results may differ from a plain program's by a relative error of at most 0.025.
Values may be sent and summed in bfloat16 or wider, within the bound.
No kernel may reach another device: no remote copies, remote signals or barrier semaphores. Data moves between devices by JAX's collectives and lax.ppermute only.
A program may use at most 192 MiB of HBM per device.

v0:
```python
import jax
import jax.numpy as jnp
from jax import lax
from jax.sharding import PartitionSpec as P

eps = 1e-06
lru_power = 8.0


def shifted(block, axis, distance):
    devices = range(lax.axis_size(axis))
    route = [(i - distance, i) for i in devices if i - distance in devices]
    return lax.ppermute(block, axis, route)


def carried_in(value, axis, join, neutral, backward):
    count, mine = (lax.axis_size(axis), lax.axis_index(axis))
    pieces = jax.tree.map(lambda part: lax.all_gather(part, axis), value)
    if backward:
        pieces = jax.tree.map(lambda part: part[::-1], pieces)
        mine = count - 1 - mine
    total = jax.tree.map(
        lambda part, zero: jnp.full_like(part, 0) + jnp.asarray(zero, part.dtype), value, neutral
    )

    def step(position, total):
        longer = join(total, jax.tree.map(lambda part: part[position], pieces))
        return jax.tree.map(lambda new, old: jnp.where(position < mine, new, old), longer, total)

    return lax.fori_loop(0, count - 1, step, total)


def rms_scale(v, gain):
    return v * lax.rsqrt(jnp.mean(v * v, axis=-1, keepdims=True) + eps) * gain


def link(earlier, later):
    return (earlier[0] * later[0], later[0] * earlier[1] + later[1])


def gelu_tanh(v):
    return jax.nn.gelu(v, approximate=True)


def gelu_glu(gate, upper):
    return gelu_tanh(gate) * upper


def recur_gates(apre, ipre, cvals, lam, flags):
    rgate = jax.nn.sigmoid(apre)
    igate = jax.nn.sigmoid(ipre)
    loga = -lru_power * rgate * jax.nn.softplus(-lam)
    keep = 1.0 - flags
    mult = flags + keep * jnp.sqrt(-jnp.expm1(2.0 * loga))
    return (jnp.exp(loga) * keep, mult * igate * cvals)


def body(
    stream,
    prescale,
    gelumat,
    gelubias,
    lrumat,
    lrubias,
    convtaps,
    convbias,
    recgates,
    recbias,
    inpgates,
    inpbias,
    lambdas,
    outmat,
    midscale,
    gatemat,
    upmatrix,
    downmat,
    resets,
    cotangent,
):
    x, g1, wy, by, wx, bx = (stream, prescale, gelumat, gelubias, lrumat, lrubias)
    conv_w, conv_b, wa, ba, wi, bi = (convtaps, convbias, recgates, recbias, inpgates, inpbias)
    lam, wo, g2, wg, wu, wd = (lambdas, outmat, midscale, gatemat, upmatrix, downmat)
    f32 = jnp.float32
    bf16 = jnp.bfloat16
    rows = x.shape[0]
    width = wy.shape[1]
    blocks = wa.shape[0]
    side = wa.shape[1]
    span = conv_w.shape[0]
    flags = resets.astype(f32)[:, None]
    keep = 1.0 - flags
    xf = x.astype(f32)
    n1f, norm_one_back = jax.vjp(rms_scale, xf, g1)
    n1 = n1f.astype(bf16)
    ypre = jnp.dot(n1, wy, preferred_element_type=f32) + by
    ucast = (jnp.dot(n1, wx, preferred_element_type=f32) + bx).astype(bf16)
    tail = jnp.flip(jnp.cumprod(jnp.flip(keep[rows - (span - 2) :], 0), 0), 0)
    edge_mask = jnp.concatenate([tail, jnp.ones((1, 1), f32)], 0)
    edge = (ucast[rows - (span - 1) :].astype(f32) * edge_mask).astype(bf16)
    borrowed = shifted(edge, "seq", 1)
    extended = jnp.concatenate([borrowed, ucast], 0).astype(f32)
    kpad = jnp.concatenate([jnp.ones((span - 1, 1), f32), keep], 0)
    conv = conv_b + conv_w[0] * extended[span - 1 :]
    alive = jnp.ones_like(keep)
    masks = [alive]
    for shift_k in range(1, span):
        alive = alive * kpad[span - shift_k : span - shift_k + rows]
        masks.append(alive)
        conv = (
            conv
            + conv_w[shift_k] * extended[span - 1 - shift_k : span - 1 - shift_k + rows] * alive
        )
    cvals = conv.astype(bf16)
    cblocks = cvals.reshape(rows, blocks, side)
    apre = (
        jnp.einsum("thk,hkj->thj", cblocks, wa, preferred_element_type=f32).reshape(rows, width)
        + ba
    )
    ipre = (
        jnp.einsum("thk,hkj->thj", cblocks, wi, preferred_element_type=f32).reshape(rows, width)
        + bi
    )

    def gate_piece(apre_v, ipre_v, c_v, lam_v):
        return recur_gates(apre_v, ipre_v, c_v, lam_v, flags)

    (carry, drive), gates_back = jax.vjp(gate_piece, apre, ipre, cvals.astype(f32), lam)
    part_p, part_h = lax.associative_scan(link, (carry, drive), axis=0)
    identity = (jnp.ones((width,), f32), jnp.zeros((width,), f32))
    into_p, into_h = carried_in((part_p[-1], part_h[-1]), "seq", link, identity, False)
    state = part_h + part_p * into_h
    yvals, gelu_back = jax.vjp(gelu_tanh, ypre)
    gated = (yvals * state).astype(bf16)
    rec = lax.psum(
        jnp.dot(gated, wo, preferred_element_type=f32).astype(jnp.bfloat16), "head"
    ).astype(jnp.float32)
    x2 = xf + rec
    n2f, norm_two_back = jax.vjp(rms_scale, x2, g2)
    n2 = n2f.astype(bf16)
    gpre = jnp.dot(n2, wg, preferred_element_type=f32)
    upm = jnp.dot(n2, wu, preferred_element_type=f32)
    hidf, glu_back = jax.vjp(gelu_glu, gpre, upm)
    hidden = hidf.astype(bf16)
    mlp = lax.psum(
        jnp.dot(hidden, wd, preferred_element_type=f32).astype(jnp.bfloat16), "head"
    ).astype(jnp.float32)
    result = (x2 + mlp).astype(bf16)
    d_hid = jnp.einsum("td,fd->tf", cotangent, wd, preferred_element_type=f32)
    d_wd = jnp.einsum("tf,td->fd", hidden, cotangent, preferred_element_type=f32)
    d_gpre, d_upm = glu_back(d_hid)
    gate_low = d_gpre.astype(bf16)
    up_low = d_upm.astype(bf16)
    d_wg = jnp.einsum("td,tf->df", n2, gate_low, preferred_element_type=f32)
    d_wu = jnp.einsum("td,tf->df", n2, up_low, preferred_element_type=f32)
    d_n2_part = jnp.einsum("tf,df->td", gate_low, wg, preferred_element_type=f32) + jnp.einsum(
        "tf,df->td", up_low, wu, preferred_element_type=f32
    )
    d_n2 = lax.psum(d_n2_part.astype(jnp.bfloat16), "head").astype(jnp.float32)
    d_x2n, d_g2 = norm_two_back(d_n2)
    d_x2 = cotangent.astype(f32) + d_x2n
    d_rec = d_x2.astype(bf16)
    d_wo = jnp.einsum("tr,td->rd", gated, d_rec, preferred_element_type=f32)
    d_gated = jnp.einsum("td,rd->tr", d_rec, wo, preferred_element_type=f32)
    d_y = d_gated * state
    d_state = d_gated * yvals
    (d_ypre,) = gelu_back(d_y)
    branch_low = d_ypre.astype(bf16)
    next_carry = jnp.concatenate([carry[1:], jnp.ones((1, width), f32)], 0)
    back_p, back_h = lax.associative_scan(link, (next_carry, d_state), axis=0, reverse=True)
    leaving = (carry[0] * back_p[0], carry[0] * back_h[0])
    from_p, from_right = carried_in(leaving, "seq", link, identity, True)
    adjoint = back_h + back_p * from_right
    prior = jnp.concatenate([into_h[None], state[:-1]], 0)
    d_apre, d_ipre, d_cdirect, d_lam = gates_back((adjoint * prior, adjoint))
    apre_low = d_apre.astype(bf16)
    ipre_low = d_ipre.astype(bf16)
    apre_blocks = apre_low.reshape(rows, blocks, side)
    ipre_blocks = ipre_low.reshape(rows, blocks, side)
    d_cvals = (
        d_cdirect
        + jnp.einsum("thj,hkj->thk", apre_blocks, wa, preferred_element_type=f32).reshape(
            rows, width
        )
        + jnp.einsum("thj,hkj->thk", ipre_blocks, wi, preferred_element_type=f32).reshape(
            rows, width
        )
    )
    d_wa = jnp.einsum("thk,thj->hkj", cblocks, apre_blocks, preferred_element_type=f32)
    d_wi = jnp.einsum("thk,thj->hkj", cblocks, ipre_blocks, preferred_element_type=f32)
    d_ba = jnp.sum(apre_low.astype(f32), 0)
    d_bi = jnp.sum(ipre_low.astype(f32), 0)
    d_conv_b = jnp.sum(d_cvals, 0)
    tap_grads = [jnp.sum(d_cvals * extended[span - 1 :], 0)]
    d_ext = jnp.pad(conv_w[0] * d_cvals, ((span - 1, 0), (0, 0)))
    for shift_k in range(1, span):
        masked = d_cvals * masks[shift_k]
        tap_grads.append(
            jnp.sum(masked * extended[span - 1 - shift_k : span - 1 - shift_k + rows], 0)
        )
        d_ext = d_ext + jnp.pad(conv_w[shift_k] * masked, ((span - 1 - shift_k, shift_k), (0, 0)))
    d_conv_w = jnp.stack(tap_grads, 0)
    returned = shifted(d_ext[: span - 1], "seq", -1)
    d_u = d_ext[span - 1 :] + jnp.pad(returned * edge_mask, ((rows - span + 1, 0), (0, 0)))
    input_low = d_u.astype(bf16)
    d_wy = jnp.einsum("td,tr->dr", n1, branch_low, preferred_element_type=f32)
    d_wx = jnp.einsum("td,tr->dr", n1, input_low, preferred_element_type=f32)
    d_by = jnp.sum(branch_low.astype(f32), 0)
    d_bx = jnp.sum(input_low.astype(f32), 0)
    d_n1_part = jnp.einsum("tr,dr->td", branch_low, wy, preferred_element_type=f32) + jnp.einsum(
        "tr,dr->td", input_low, wx, preferred_element_type=f32
    )
    d_n1 = lax.psum(d_n1_part.astype(jnp.bfloat16), "head").astype(jnp.float32)
    d_xn, d_g1 = norm_one_back(d_n1)
    d_x = (d_x2 + d_xn).astype(bf16)
    d_by, d_bx, d_conv_w, d_conv_b, d_wa, d_ba, d_wi, d_bi, d_lam = (
        lax.psum(d_by.astype(jnp.bfloat16), "seq").astype(jnp.float32),
        lax.psum(d_bx.astype(jnp.bfloat16), "seq").astype(jnp.float32),
        lax.psum(d_conv_w.astype(jnp.bfloat16), "seq").astype(jnp.float32),
        lax.psum(d_conv_b.astype(jnp.bfloat16), "seq").astype(jnp.float32),
        lax.psum(d_wa.astype(jnp.bfloat16), "seq").astype(jnp.float32),
        lax.psum(d_ba.astype(jnp.bfloat16), "seq").astype(jnp.float32),
        lax.psum(d_wi.astype(jnp.bfloat16), "seq").astype(jnp.float32),
        lax.psum(d_bi.astype(jnp.bfloat16), "seq").astype(jnp.float32),
        lax.psum(d_lam.astype(jnp.bfloat16), "seq").astype(jnp.float32),
    )
    d_wy, d_wx, d_wo, d_g1, d_wg, d_wu, d_wd, d_g2 = (
        lax.psum_scatter(d_wy.astype(jnp.bfloat16), "seq", scatter_dimension=0, tiled=True).astype(
            jnp.float32
        ),
        lax.psum_scatter(d_wx.astype(jnp.bfloat16), "seq", scatter_dimension=0, tiled=True).astype(
            jnp.float32
        ),
        lax.psum_scatter(d_wo.astype(jnp.bfloat16), "seq", scatter_dimension=1, tiled=True).astype(
            jnp.float32
        ),
        lax.psum_scatter(d_g1.astype(jnp.bfloat16), "seq", scatter_dimension=0, tiled=True).astype(
            jnp.float32
        ),
        lax.psum_scatter(d_wg.astype(jnp.bfloat16), "seq", scatter_dimension=0, tiled=True).astype(
            jnp.float32
        ),
        lax.psum_scatter(d_wu.astype(jnp.bfloat16), "seq", scatter_dimension=0, tiled=True).astype(
            jnp.float32
        ),
        lax.psum_scatter(d_wd.astype(jnp.bfloat16), "seq", scatter_dimension=1, tiled=True).astype(
            jnp.float32
        ),
        lax.psum_scatter(d_g2.astype(jnp.bfloat16), "seq", scatter_dimension=0, tiled=True).astype(
            jnp.float32
        ),
    )
    return (
        result,
        d_x,
        d_g1,
        d_wy,
        d_by,
        d_wx,
        d_bx,
        d_conv_w,
        d_conv_b,
        d_wa,
        d_ba,
        d_wi,
        d_bi,
        d_lam,
        d_wo,
        d_g2,
        d_wg,
        d_wu,
        d_wd,
    )


def solution(mesh):
    in_specs = (
        P("seq", None),
        P(),
        P(None, "head"),
        P("head"),
        P(None, "head"),
        P("head"),
        P(None, "head"),
        P("head"),
        P("head", None, None),
        P("head"),
        P("head", None, None),
        P("head"),
        P("head"),
        P("head", None),
        P(),
        P(None, "head"),
        P(None, "head"),
        P("head", None),
        P("seq"),
        P("seq", None),
    )
    out_specs = (
        P("seq", None),
        P("seq", None),
        P("seq"),
        P("seq", "head"),
        P("head"),
        P("seq", "head"),
        P("head"),
        P(None, "head"),
        P("head"),
        P("head", None, None),
        P("head"),
        P("head", None, None),
        P("head"),
        P("head"),
        P("head", "seq"),
        P("seq"),
        P("seq", "head"),
        P("seq", "head"),
        P("head", "seq"),
    )
    return jax.shard_map(body, mesh=mesh, in_specs=in_specs, out_specs=out_specs, check_vma=False)
```

profile of v0, /device:TPU:0, one launch (start us, length us, event | category | flops | bytes accessed | tf_op | source)
XLA Modules:
  0.0 1758.5 jit_solution(9346374829386691861)
XLA Ops:
  46.1 9.6 convert_multiply_fusion.9
  57.5 6.3 slice.757
  63.9 6.3 slice.687
  70.1 6.2 slice.686
  77.7 6.2 slice.689
  83.9 6.3 slice.685
  204.7 6.3 slice.684
  337.4 8.5 pad.306
  348.6 8.6 pad.286
  362.9 8.5 pad.305
  372.2 10.9 all-gather
  386.1 8.6 pad.285
  395.4 8.0 all-gather.1
  404.0 5.4 while.28
  409.5 9.4 multiply_convert_fusion.3
  423.4 121.4 %all-reduce.98.cloned.1.call-done = bf16[1024,1536]{1,0:T(8,128)(2,1)} async-done(((bf16[1024,1536]{1,0:T(8,128)(2,1)}), bf16[1024,1536]{1,0:T(8,128)(2,1)}) %all-reduce.98.cloned.1.call-update) | async-done | bytes 3145744 | tf_op jit(solution)/shard_map/psum | solution.py:134
  555.8 6.2 fusion.112
  562.1 10.4 multiply_convert_fusion.1
  576.7 5.7 add_convert_fusion.1
  585.9 6.5 slice.790
  592.4 6.3 slice.783
  598.6 6.2 slice.781
  604.9 8.9 slice.791
  613.8 9.1 slice.782
  622.9 8.9 slice.784
  631.8 71.0 %all-reduce.100.cloned.1.call-done = bf16[1024,1536]{1,0:T(8,128)(2,1)} async-done(((bf16[1024,1536]{1,0:T(8,128)(2,1)}), bf16[1024,1536]{1,0:T(8,128)(2,1)}) %all-reduce.100.cloned.1.call-update) | async-done | bytes 3145744 | tf_op jit(solution)/shard_map/psum | solution.py:158
  702.8 6.9 fusion.6
  713.9 4.7 fusion.95
  721.3 6.2 slice.859
  727.5 6.3 slice.787
  733.8 6.2 slice.785
  740.0 8.9 slice.786
  748.9 8.9 slice.788
  873.2 9.1 slice.860
  985.2 4.6 pad.323
  1001.0 4.6 pad.324
  1013.8 8.5 pad.325
  1022.3 8.7 pad.345
  1031.0 8.6 pad.346
  1039.6 8.6 pad.326
  1055.5 16.6 rev.23
  1072.2 16.6 rev.24
  1088.7 9.0 all-gather.3
  1100.9 8.7 all-gather.2
  1112.8 5.4 while.29
  1118.4 12.0 multiply_reduce_fusion.1
  1131.2 5.3 fusion.91
  1140.1 8.7 convolution_convert_fusion
  1148.9 8.7 convolution_convert_fusion.2
  1157.8 8.7 convolution_convert_fusion.1
  1166.6 6.2 convolution_convert_fusion.5
  1184.6 5.3 convolution_convert_fusion.7
  1190.0 9.6 multiply_reduce_fusion.5
  1209.0 7.4 convolution_convert_fusion.4
  1229.6 13.2 reduce-scatter.17.cloned.1.call-done
  1244.8 49.9 %reduce-scatter.13.cloned.1.call-done = bf16[192,1152]{1,0:T(8,128)(2,1)} async-done(((bf16[1536,1152]{1,0:T(8,128)(2,1)}), bf16[192,1152]{1,0:T(8,128)(2,1)}) %reduce-scatter.13.cloned.1.call-update) | async-done | bytes 442384 | tf_op jit(solution)/shard_map/reduce_scatter | solution.py:239
  1296.7 49.9 %reduce-scatter.15.cloned.1.call-done = bf16[192,1152]{1,0:T(8,128)(2,1)} async-done(((bf16[1536,1152]{1,0:T(8,128)(2,1)}), bf16[192,1152]{1,0:T(8,128)(2,1)}) %reduce-scatter.15.cloned.1.call-update) | async-done | bytes 442384 | tf_op jit(solution)/shard_map/reduce_scatter | solution.py:242
  1348.6 40.1 %reduce-scatter.11.cloned.1.call-done = bf16[512,192]{0,1:T(8,128)(2,1)} async-done(((bf16[512,1536]{0,1:T(8,128)(2,1)}), bf16[512,192]{0,1:T(8,128)(2,1)}) %reduce-scatter.11.cloned.1.call-update) | async-done | bytes 196624 | tf_op jit(solution)/shard_map/reduce_scatter | solution.py:233
  1390.4 40.4 %reduce-scatter.7.cloned.1.call-done = bf16[192,512]{1,0:T(8,128)(2,1)} async-done(((bf16[1536,512]{1,0:T(8,128)(2,1)}), bf16[192,512]{1,0:T(8,128)(2,1)}) %reduce-scatter.7.cloned.1.call-update) | async-done | bytes 196624 | tf_op jit(solution)/shard_map/reduce_scatter | solution.py:227
  1432.5 40.4 %reduce-scatter.9.cloned.1.call-done = bf16[192,512]{1,0:T(8,128)(2,1)} async-done(((bf16[1536,512]{1,0:T(8,128)(2,1)}), bf16[192,512]{1,0:T(8,128)(2,1)}) %reduce-scatter.9.cloned.1.call-update) | async-done | bytes 196624 | tf_op jit(solution)/shard_map/reduce_scatter | solution.py:230
  1474.7 224.5 %all-reduce.104.cloned.1.call-done = (bf16[1024,1536]{1,0:T(8,128)(2,1)}, bf16[1024,1536]{1,0:T(8,128)(2,1)}) async-done(((bf16[1024,1536]{1,0:T(8,128)(2,1)}, bf16[1024,1536]{1,0:T(8,128)(2,1)}), (bf16[1024,1536]{1,0:T(8,128)(2,1)}, bf16[1024,1536]{1,0:T(8,128)(2,1)})) %all-reduce.104.cloned.1.call-update) | async-done | bytes 6291472 | tf_op jit(solution)/shard_map/psum | solution.py:144
  1699.2 5.2 fusion.7
  1705.0 25.3 %all-reduce.90 = (bf16[1536]{0:T(1024)(128)(2,1)}, bf16[512]{0:T(512)(128)(2,1)}, bf16[512]{0:T(512)(128)(2,1)}, bf16[4,512]{1,0:T(4,128)(2,1)}, bf16[512]{0:T(5...) all-reduce(bf16[1536]{0:T(1024)(128)(2,1)} %get-tuple-element.247, ...), channel_id=2, replica_groups=mesh['seq'=8,'head'=4] {'seq'}, use_global_device_ids=true, to_apply=%region_14.15.clone | all-reduce | flops 8192 | bytes 32768
  1741.6 9.8 fusion.10
  (702 shorter events, 649.3 us)
Async XLA Ops:
  7.2 554.9 %copy-start = (bf16[1152,1536]{1,0:T(8,128)(2,1)S(1)}, bf16[1152,1536]{1,0:T(8,128)(2,1)}, u32[]{:S(2)}) copy-start(bf16[1152,1536]{1,0:T(8,128)(2,1)} %param.41) | copy-start | bytes 10616836
  7.2 8.2 copy-start.91
  7.2 8.2 copy-start.130
  7.2 537.7 %all-reduce.98.cloned.1.call-start = ((), (), s32[]{:S(2)}) async-start(), calls=%async_computation.6 | async-start | bytes 6291456 | tf_op jit(solution)/shard_map/psum | solution.py:134
  8.1 37.9 %copy-start.57 = (f32[1024]{0:T(1024)}, f32[1024]{0:T(1024)S(1)}, u32[]{:S(2)}) copy-start(f32[1024]{0:T(1024)S(1)} %broadcast_subtract_fusion) | copy-start | bytes 12292
  15.4 7.9 copy-start.117
  15.4 8.6 copy-start.115
  20.3 5.5 collective-permute-start
  23.9 22.2 %copy-start.71 = (f32[1,512]{1,0:T(1,128)}, f32[1,512]{1,0:T(1,128)S(1)}, u32[]{:S(2)}) copy-start(f32[1,512]{1,0:T(1,128)S(1)} %get-tuple-element.394) | copy-start | bytes 6148
  24.0 22.1 %copy-start.61 = (f32[1024,1]{0,1:T(1,128)}, f32[1024,1]{0,1:T(1,128)S(1)}, u32[]{:S(2)}) copy-start(f32[1024,1]{0,1:T(1,128)S(1)} %get-tuple-element.301) | copy-start | bytes 12292
  24.0 22.1 %copy-start.63 = (f32[1024,1]{0,1:T(1,128)}, f32[1024,1]{0,1:T(1,128)S(1)}, u32[]{:S(2)}) copy-start(f32[1024,1]{0,1:T(1,128)S(1)} %get-tuple-element.302) | copy-start | bytes 12292
  237.6 26.9 %copy-start.113 = (f32[1,512]{1,0:T(1,128)S(1)}, f32[1,512]{1,0:T(1,128)}, u32[]{:S(2)}) copy-start(f32[1,512]{1,0:T(1,128)} %slice.893) | copy-start | bytes 6148
  249.0 28.7 %copy-start.111 = (f32[1,512]{1,0:T(1,128)S(1)}, f32[1,512]{1,0:T(1,128)}, u32[]{:S(2)}) copy-start(f32[1,512]{1,0:T(1,128)} %slice.924) | copy-start | bytes 6148
  258.0 22.8 %copy-start.109 = (f32[1,512]{1,0:T(1,128)S(1)}, f32[1,512]{1,0:T(1,128)}, u32[]{:S(2)}) copy-start(f32[1,512]{1,0:T(1,128)} %slice.892) | copy-start | bytes 6148
  287.0 8.1 copy-start.107
  291.1 7.3 copy-start.105
  362.9 20.8 %copy-start.98 = (f32[1,512]{1,0:T(1,128)S(1)}, f32[1,512]{1,0:T(1,128)}, u32[]{:S(2)}) copy-start(f32[1,512]{1,0:T(1,128)} %slice.889) | copy-start | bytes 6148
  386.1 17.9 %copy-start.68 = (f32[512]{0:T(512)S(1)}, f32[512]{0:T(512)}, u32[]{:S(2)}) copy-start(f32[512]{0:T(512)} %custom-call) | copy-start | bytes 6148
  386.1 23.4 %copy-start.88 = (f32[1024]{0:T(1024)S(1)}, f32[1024]{0:T(1024)}, u32[]{:S(2)}) copy-start(f32[1024]{0:T(1024)} %copy-done.87) | copy-start | bytes 12292
  386.1 23.4 %copy-start.92 = (f32[1536]{0:T(1024)S(1)}, f32[1536]{0:T(1024)}, u32[]{:S(2)}) copy-start(f32[1536]{0:T(1024)} %param.25) | copy-start | bytes 18436
  409.4 9.5 copy-start.69
  409.4 10.4 copy-start.127
  423.4 125.6 %copy-start.70 = (f32[1536]{0:T(1024)S(1)}, f32[1536]{0:T(1024)}, u32[]{:S(2)}) copy-start(f32[1536]{0:T(1024)} %param.38) | copy-start | bytes 18436
  423.4 279.4 %all-reduce.100.cloned.1.call-start = ((), (), s32[]{:S(2)}) async-start(), calls=%async_computation.7 | async-start | bytes 6291456 | tf_op jit(solution)/shard_map/psum | solution.py:158
  582.5 643.9 %all-reduce.102.cloned.1.call-start = ((), (), s32[]{:S(2)}) async-start(), calls=%async_computation.14 | async-start | bytes 524288 | tf_op jit(solution)/shard_map/psum | solution.py:220
  702.7 7.0 copy-start.15
  872.6 9.7 copy-start.118
  872.6 9.7 copy-start.119
  908.4 27.0 %copy-start.114 = (f32[1,512]{1,0:T(1,128)S(1)}, f32[1,512]{1,0:T(1,128)}, u32[]{:S(2)}) copy-start(f32[1,512]{1,0:T(1,128)} %slice.989) | copy-start | bytes 6148
  919.8 28.8 %copy-start.112 = (f32[1,512]{1,0:T(1,128)S(1)}, f32[1,512]{1,0:T(1,128)}, u32[]{:S(2)}) copy-start(f32[1,512]{1,0:T(1,128)} %slice.957) | copy-start | bytes 6148
  928.8 22.8 %copy-start.110 = (f32[1,512]{1,0:T(1,128)S(1)}, f32[1,512]{1,0:T(1,128)}, u32[]{:S(2)}) copy-start(f32[1,512]{1,0:T(1,128)} %slice.988) | copy-start | bytes 6148
  957.9 8.1 copy-start.108
  962.0 7.4 copy-start.106
  1072.2 40.6 %copy-start.67 = (f32[512]{0:T(512)S(1)}, f32[512]{0:T(512)}, u32[]{:S(2)}) copy-start(f32[512]{0:T(512)} %custom-call.1) | copy-start | bytes 6148
  1072.2 46.0 %copy-start.58 = (f32[1024]{0:T(1024)S(1)}, f32[1024]{0:T(1024)}, u32[]{:S(2)}) copy-start(f32[1024]{0:T(1024)} %copy-done.57) | copy-start | bytes 12292
  1072.2 46.0 %copy-start.62 = (f32[1024,1]{0,1:T(1,128)S(1)}, f32[1024,1]{0,1:T(1,128)}, u32[]{:S(2)}) copy-start(f32[1024,1]{0,1:T(1,128)} %copy-done.61) | copy-start | bytes 12292
  1072.2 46.1 %copy-start.64 = (f32[1024,1]{0,1:T(1,128)S(1)}, f32[1024,1]{0,1:T(1,128)}, u32[]{:S(2)}) copy-start(f32[1024,1]{0,1:T(1,128)} %copy-done.63) | copy-start | bytes 12292
  1118.2 12.2 copy-start.116
  1118.2 12.8 copy-start.2
  1118.2 12.8 copy-start.9
  1118.3 12.8 copy-start.10
  1118.3 12.8 copy-start.72
  1118.3 12.8 copy-start.75
  1118.3 12.8 copy-start.78
  1118.3 12.8 copy-start.81
  1118.3 12.8 copy-start.83
  1118.3 12.8 copy-start.84
  1118.3 12.8 copy-start.94
  1118.3 12.8 copy-start.95
  1118.4 12.8 copy-start.96
  1139.7 103.2 %reduce-scatter.17.cloned.1.call-start = ((), (), s32[]{:S(2)}) async-start(), calls=%async_computation.13 | async-start | bytes 3981312 | tf_op jit(solution)/shard_map/reduce_scatter | solution.py:245
  1148.8 145.9 %reduce-scatter.13.cloned.1.call-start = ((), (), s32[]{:S(2)}) async-start(), calls=%async_computation.11 | async-start | bytes 3981312 | tf_op jit(solution)/shard_map/reduce_scatter | solution.py:239
  1157.6 189.0 %reduce-scatter.15.cloned.1.call-start = ((), (), s32[]{:S(2)}) async-start(), calls=%async_computation.12 | async-start | bytes 3981312 | tf_op jit(solution)/shard_map/reduce_scatter | solution.py:242
  1166.5 222.2 %reduce-scatter.11.cloned.1.call-start = ((), (), s32[]{:S(2)}) async-start(), calls=%async_computation.10 | async-start | bytes 1769472 | tf_op jit(solution)/shard_map/reduce_scatter | solution.py:233
  1172.7 258.0 %reduce-scatter.7.cloned.1.call-start = ((), (), s32[]{:S(2)}) async-start(), calls=%async_computation.8 | async-start | bytes 1769472 | tf_op jit(solution)/shard_map/reduce_scatter | solution.py:227
  1189.9 9.7 copy-start.73
  1189.9 283.0 %reduce-scatter.9.cloned.1.call-start = ((), (), s32[]{:S(2)}) async-start(), calls=%async_computation.9 | async-start | bytes 1769472 | tf_op jit(solution)/shard_map/reduce_scatter | solution.py:230
  1190.0 9.6 copy-start.76
  1190.0 9.6 copy-start.79
  1190.0 9.6 copy-start.82
  1200.5 3.1 collective-permute-start.1
  1208.9 490.2 %all-reduce.104.cloned.1.call-start = ((), (), s32[]{:S(2)}) async-start(), calls=%async_computation.15 | async-start | bytes 12582912 | tf_op jit(solution)/shard_map/psum | solution.py:144
  1209.0 7.4 copy-start.129
  1209.0 7.4 copy-start.132
  (84 other events, 260.8 us)
Sparse Core Ops, SparseCore 0:
  423.5 121.3 all-reduce.97
  582.6 120.0 all-reduce.99
  1139.8 51.7 all-reduce.101
  1195.4 47.4 reduce-scatter.16
  1246.6 48.0 reduce-scatter.12
  1298.5 48.0 reduce-scatter.14
  1350.2 38.4 reduce-scatter.10
  1392.3 38.4 reduce-scatter.6
  1434.4 38.4 reduce-scatter.8
  1475.9 223.1 all-reduce.103
where the time goes:
time: 1780 us; the launch traced here: 1760 us
  waiting for transfers between devices  651 us (37%)
  local copies, waits for them, and re-layouts  629 us (35%)
  other arithmetic  275 us (15%)
  matrix products  119 us (7%)
  blocking collectives  61.8 us (3%)
    psum x1, waiting for transfers between devices, body(): lax.psum(jnp.dot(hidden, wd, preferred_element_type=f32).astype(jnp.bfloa...  224 us
    slice x73, local copies, waits for them, and re-layouts, body(): lax.associative_scan(link, (next_carry, d_state), axis=0, reverse=True)  185 us
    slice x68, local copies, waits for them, and re-layouts, body(): part_p, part_h = lax.associative_scan(link, (carry, drive), axis=0)  133 us
    psum x1, waiting for transfers between devices, body(): lax.psum(jnp.dot(gated, wo, preferred_element_type=f32).astype(jnp.bfloat...  121 us
    pad x36, local copies, waits for them, and re-layouts, body(): lax.associative_scan(link, (next_carry, d_state), axis=0, reverse=True)  107 us
    pad x36, local copies, waits for them, and re-layouts, body(): part_p, part_h = lax.associative_scan(link, (carry, drive), axis=0)  106 us
    psum x1, waiting for transfers between devices, body(): d_n2 = lax.psum(d_n2_part.astype(jnp.bfloat16), 'head').astype(jnp.float32)  71 us
    reduce_scatter x1, waiting for transfers between devices, body(): lax.psum_scatter(d_wu.astype(jnp.bfloat16), 'seq', scatter_dimension=0, t...  49.9 us
  transfers between devices with their start and end apart: 12, of which 10 were waited for; matrix products, arithmetic and copies ran while one was open for 8% of the time, Pallas kernels for 0%

commit v1 on v0

v1 whole, which is shorter than its diff:
```python
import functools
import jax
import jax.numpy as jnp
from jax import lax
from jax.experimental import pallas as pl
from jax.experimental.pallas import tpu as pltpu
from jax.sharding import PartitionSpec as P

f32 = jnp.float32
bf16 = jnp.bfloat16
EPS = 1e-06
POWER = 8.0
HALO = 16
SEGS = 8
MIB = 1 << 20
ROOT = 0.7978845608028654
CUBE = 0.044715


def dot(a, b):
    return jnp.dot(a, b, preferred_element_type=f32)


def dot_nt(a, b):
    return lax.dot_general(a, b, (((1,), (1,)), ((), ())), preferred_element_type=f32)


def dot_tn(a, b):
    return lax.dot_general(a, b, (((0,), (0,)), ((), ())), preferred_element_type=f32)


def whole(shape):
    return pl.BlockSpec(shape, lambda *i: (0,) * len(shape))


def params(mib):
    return pltpu.CompilerParams(
        dimension_semantics=("arbitrary",), vmem_limit_bytes=mib * MIB
    )


def sds(shape, dtype):
    return jax.ShapeDtypeStruct(shape, dtype)


def one_minus_exp(z):
    s = 1.0 - z * (1.0 / 8.0)
    for n in (7.0, 6.0, 5.0, 4.0, 3.0, 2.0):
        s = 1.0 - (z * (1.0 / n)) * s
    return z * s


def gelu(v):
    th = jnp.tanh(ROOT * (v + CUBE * v * v * v))
    return 0.5 * v * (1.0 + th)


def gelu_both(v):
    sq = v * v
    th = jnp.tanh(ROOT * v * (1.0 + CUBE * sq))
    half = 0.5 * (1.0 + th)
    slope = half + 0.5 * v * (1.0 - th * th) * (ROOT * (1.0 + 3.0 * CUBE * sq))
    return v * half, slope


def recur_kernel(
    x_ref, xe_ref, m_ref, wy_ref, wx_ref, vec_ref, g1_ref, wai_ref,
    n1_ref, ypre_ref, u_ref, c_ref, carry_ref, r_ref, i_ref, h_ref, p_ref, end_ref, ue_ref,
    uext, cbuf, dbuf, hs, ps, run,
):
    tb, width = x_ref.shape
    chan = wy_ref.shape[1]
    length = tb // SEGS
    b = pl.program_id(0)
    vec = lambda k: vec_ref[k : k + 1, :]

    def norm(v):
        v = v.astype(f32)
        ms = jnp.mean(v * v, axis=-1, keepdims=True)
        return (v * lax.rsqrt(ms + EPS) * g1_ref[...]).astype(bf16)

    @pl.when(b == 0)
    def _():
        ne = norm(xe_ref[:, :width])
        ue = (dot(ne, wx_ref[...]) + vec(1)).astype(bf16).astype(f32)
        ue = ue * xe_ref[:, width : width + 1].astype(f32)
        uext[:HALO, :] = ue
        ue_ref[...] = ue
        run[0:1, :] = jnp.ones((1, chan), f32)
        run[1:2, :] = jnp.zeros((1, chan), f32)

    @pl.when(b > 0)
    def _():
        uext[:HALO, :] = uext[tb : tb + HALO, :]

    n1 = norm(x_ref[...])
    n1_ref[...] = n1
    u = (dot(n1, wx_ref[...]) + vec(1)).astype(bf16)
    u_ref[...] = u
    uext[HALO:, :] = u.astype(f32)
    ypre_ref[...] = dot(n1, wy_ref[...]) + vec(0)
    keep = m_ref[:, 0:1]
    alive2 = m_ref[:, 1:2]
    alive3 = m_ref[:, 2:3]
    side = wai_ref.shape[1]
    for k in range(chan // side):
        ln = slice(k * side, (k + 1) * side)
        v = lambda j: vec_ref[j : j + 1, ln]
        conv = v(6) + v(2) * uext[HALO:, ln]
        conv = conv + v(3) * uext[HALO - 1 : HALO - 1 + tb, ln] * keep
        conv = conv + v(4) * uext[HALO - 2 : HALO - 2 + tb, ln] * alive2
        conv = conv + v(5) * uext[HALO - 3 : HALO - 3 + tb, ln] * alive3
        c = conv.astype(bf16)
        c_ref[:, ln] = c
        g = dot(c, wai_ref[k])
        r = jax.nn.sigmoid(g[:, :side] + v(7))
        i = jax.nn.sigmoid(g[:, side:] + v(8))
        r_ref[:, ln] = r
        i_ref[:, ln] = i
        decay = r * v(9)
        mult = (1.0 - keep) + keep * jnp.sqrt(one_minus_exp(2.0 * decay))
        carry = jnp.exp(-decay) * keep
        carry_ref[:, ln] = carry
        cbuf[k] = carry
        dbuf[k] = mult * i * c.astype(f32)
    blocks = chan // 128
    hh = [jnp.zeros((SEGS, 128), f32) for _ in range(blocks)]
    pp = [jnp.ones((SEGS, 128), f32) for _ in range(blocks)]
    for j in range(length):
        rows = pl.ds(j, SEGS, stride=length)
        for k in range(blocks):
            a = cbuf[k, rows, :]
            hh[k] = a * hh[k] + dbuf[k, rows, :]
            pp[k] = a * pp[k]
            hs[k, rows, :] = hh[k]
            ps[k, rows, :] = pp[k]
    for k in range(blocks):
        ln = slice(k * 128, (k + 1) * 128)
        prow = run[0:1, ln]
        hrow = run[1:2, ln]
        for s in range(SEGS):
            rows = slice(s * length, (s + 1) * length)
            pseg = ps[k, rows, :]
            h_ref[rows, ln] = hs[k, rows, :] + pseg * hrow
            p_ref[rows, ln] = pseg * prow
            hrow = hh[k][s : s + 1, :] + pp[k][s : s + 1, :] * hrow
            prow = pp[k][s : s + 1, :] * prow
        run[0:1, ln] = prow
        run[1:2, ln] = hrow
        end_ref[0:1, ln] = prow
        end_ref[1:2, ln] = hrow


def recur(x, xe, masks, wy, wx, vec, g1, wai, tb):
    rows, width = x.shape
    chan = wy.shape[1]
    rowspec = lambda w: pl.BlockSpec((tb, w), lambda b: (b, 0))
    act = [(width, bf16), (chan, f32), (chan, bf16), (chan, bf16)] + [(chan, f32)] * 5
    return pl.pallas_call(
        recur_kernel,
        grid=(rows // tb,),
        in_specs=[
            rowspec(width), whole(xe.shape), rowspec(masks.shape[1]), whole(wy.shape),
            whole(wx.shape), whole(vec.shape), whole(g1.shape), whole(wai.shape),
        ],
        out_specs=[rowspec(w) for w, _ in act] + [whole((2, chan)), whole((HALO, chan))],
        out_shape=[sds((rows, w), d) for w, d in act]
        + [sds((2, chan), f32), sds((HALO, chan), f32)],
        scratch_shapes=[
            pltpu.VMEM((tb + HALO, chan), f32),
            *[pltpu.VMEM((chan // 128, tb, 128), f32)] * 4,
            pltpu.VMEM((2, chan), f32),
        ],
        compiler_params=params(40),
        name="recur",
    )(x, xe, masks, wy, wx, vec, g1, wai)


def entering(ends_ref, mine, backward):
    count = ends_ref.shape[0]
    total = jnp.zeros_like(ends_ref[0, 1:2, :])
    for s in range(count - 1):
        at = count - 1 - s if backward else s
        new = ends_ref[at, 0:1, :] * total + ends_ref[at, 1:2, :]
        inside = at > mine if backward else at < mine
        total = jnp.where(inside, new, total)
    return total


def out_kernel(mine_ref, h_ref, p_ref, ypre_ref, ends_ref, wo_ref, *rest):
    state_ref, gl_ref, part_ref = rest[-3:]
    into = entering(ends_ref, mine_ref[0], False)
    state = h_ref[...] + p_ref[...] * into
    state_ref[...] = state
    gl = (gelu(ypre_ref[...]) * state).astype(bf16)
    gl_ref[...] = gl
    part_ref[...] = dot(gl, wo_ref[...]).astype(bf16)


SMEM = pl.BlockSpec(memory_space=pltpu.SMEM)
ANY = pl.BlockSpec(memory_space=pl.ANY)


def chunk_call(kernel, at, tb, chunked, fixed, outs, carried, extra_outs, mib, name, scratch=()):
    rows = chunked[0].shape[0]
    spec = lambda w: pl.BlockSpec((tb, w), lambda *i: (at, 0))
    carried = [] if carried is None else list(carried)
    base = len(fixed) + len(chunked)
    ins = [SMEM if a.dtype == jnp.int32 else whole(a.shape) for a in fixed]
    return pl.pallas_call(
        kernel,
        grid=(1,),
        in_specs=ins + [spec(a.shape[1]) for a in chunked] + [ANY] * len(carried),
        out_specs=[spec(w) for w, _ in outs] + [whole(s) for s, _ in extra_outs],
        out_shape=[sds((rows, w), d) for w, d in outs] + [sds(s, d) for s, d in extra_outs],
        scratch_shapes=list(scratch),
        input_output_aliases={base + k: k for k in range(len(carried))},
        compiler_params=params(mib),
        name=name,
    )(*fixed, *chunked, *carried)


def out_chunk(at, tb, mine, h, p, ypre, ends, wo, carried):
    def kernel(mine_ref, ends_ref, wo_ref, h_ref, p_ref, ypre_ref, *rest):
        out_kernel(mine_ref, h_ref, p_ref, ypre_ref, ends_ref, wo_ref, *rest)

    chan, width = wo.shape
    return chunk_call(
        kernel, at, tb, [h, p, ypre], [mine, ends, wo], [(chan, f32), (chan, bf16)],
        carried, [((tb, width), bf16)], 24, "out_proj",
    )


def slopes_kernel(
    mine_ref, ends_ref, vec_ref, r_ref, i_ref, carry_ref, c_ref, state_ref, before_ref, m_ref,
    a_ref, b_ref, d_ref, g_ref, sext,
):
    tb = r_ref.shape[0]
    b = pl.program_id(0)
    sext[8:, :] = state_ref[...]
    sext[:8, :] = before_ref[...]

    @pl.when(b == 0)
    def _():
        sext[7:8, :] = entering(ends_ref, mine_ref[0], False)

    keep = m_ref[:, 0:1]
    sp = vec_ref[9:10, :]
    r = r_ref[...]
    i = i_ref[...]
    c = c_ref[...].astype(f32)
    m2 = one_minus_exp(2.0 * (r * sp))
    m = jnp.sqrt(m2)
    mult = (1.0 - keep) + keep * m
    prior = sext[7 : 7 + tb, :]
    grad = prior * carry_ref[...] - i * c * keep * (1.0 - m2) / m
    gr = grad * r
    g_ref[...] = gr
    a_ref[...] = -gr * sp * (1.0 - r)
    mi = mult * i
    b_ref[...] = mi * c * (1.0 - i)
    d_ref[...] = mi


def slopes(mine, ends, vec, r, i, carry, c, state, masks, tb):
    rows, chan = r.shape
    spec = lambda w: pl.BlockSpec((tb, w), lambda b: (b, 0))
    before = pl.BlockSpec((8, chan), lambda b: (jnp.maximum(b * (tb // 8) - 1, 0), 0))
    return pl.pallas_call(
        slopes_kernel,
        grid=(rows // tb,),
        in_specs=[SMEM, whole(ends.shape), whole(vec.shape)]
        + [spec(chan)] * 5
        + [before, spec(masks.shape[1])],
        out_specs=[spec(chan)] * 4,
        out_shape=[sds((rows, chan), f32)] * 4,
        scratch_shapes=[pltpu.VMEM((tb + 8, chan), f32)],
        compiler_params=params(24),
        name="slopes",
    )(mine, ends, vec, r, i, carry, c, state, state, masks)


def pick(mid_ref, t_ref, far_ref):
    mid = mid_ref[0] == 1
    return jnp.where(mid, t_ref[...], far_ref[...])


def mlp_kernel(
    mid_ref, t_ref, far_ref, g2_ref, wg_ref, wu_ref, wd_ref, x_ref, cot_ref, *rest,
):
    rec_ref, n2_ref, hid_ref, dg_ref, du_ref, mpart_ref, dpart_ref, n2s, macc, dacc = rest[-10:]
    f = pl.program_id(0)

    @pl.when(f == 0)
    def _():
        rec = pick(mid_ref, t_ref, far_ref)
        rec_ref[...] = rec
        x2 = x_ref[...].astype(f32) + rec.astype(f32)
        ms = jnp.mean(x2 * x2, axis=-1, keepdims=True)
        n2 = (x2 * lax.rsqrt(ms + EPS) * g2_ref[...]).astype(bf16)
        n2s[...] = n2
        n2_ref[...] = n2

    n2 = n2s[...]
    wd = wd_ref[...]
    wg = wg_ref[...]
    wu = wu_ref[...]
    gpre = dot(n2, wg)
    up = dot(n2, wu)
    dh = dot_nt(cot_ref[...], wd)
    act, slope = gelu_both(gpre)
    hid = (act * up).astype(bf16)
    dg = (dh * up * slope).astype(bf16)
    du = (dh * act).astype(bf16)
    hid_ref[...] = hid
    dg_ref[...] = dg
    du_ref[...] = du
    mp = dot(hid, wd)
    dp = dot_nt(dg, wg) + dot_nt(du, wu)
    last = pl.num_programs(0) - 1

    @pl.when(f == 0)
    def _():
        macc[...] = mp
        dacc[...] = dp

    @pl.when((f > 0) & (f < last))
    def _():
        macc[...] += mp
        dacc[...] += dp

    @pl.when(f == last)
    def _():
        mpart_ref[...] = (macc[...] + mp).astype(bf16)
        dpart_ref[...] = (dacc[...] + dp).astype(bf16)


def mlp_chunk(at, tb, mid, t, far, g2, wg, wu, wd, x, cot, carried, fb):
    rows, width = x.shape
    hidden = wg.shape[1]
    row = lambda w: pl.BlockSpec((tb, w), lambda f: (at, 0))
    col = pl.BlockSpec((tb, fb), lambda f: (at, f))
    carried = [] if carried is None else list(carried)
    return pl.pallas_call(
        mlp_kernel,
        grid=(hidden // fb,),
        in_specs=[
            SMEM, whole(t.shape), whole(far.shape), whole(g2.shape),
            pl.BlockSpec((width, fb), lambda f: (0, f)), pl.BlockSpec((width, fb), lambda f: (0, f)),
            pl.BlockSpec((fb, width), lambda f: (f, 0)), row(width), row(width),
        ]
        + [ANY] * len(carried),
        out_specs=[row(width), row(width), col, col, col, whole((tb, width)), whole((tb, width))],
        out_shape=[sds((rows, width), bf16)] * 2
        + [sds((rows, hidden), bf16)] * 3
        + [sds((tb, width), bf16)] * 2,
        scratch_shapes=[
            pltpu.VMEM((tb, width), bf16), pltpu.VMEM((tb, width), f32), pltpu.VMEM((tb, width), f32),
        ],
        input_output_aliases={9 + k: k for k in range(len(carried))},
        compiler_params=params(40),
        name="mlp",
    )(mid, t, far, g2, wg, wu, wd, x, cot, *carried)


def back_kernel(
    mid_ref, t_ref, far_ref, g2_ref, wo_ref, run_ref,
    x_ref, rec_ref, cot_ref, state_ref, ypre_ref, carry_ref, *rest,
):
    dx2_ref, drec_ref, branch_ref, adj_ref, q_ref, end_ref, dg2_ref, cbuf, dbuf, al, ql = rest[-11:]
    tb = x_ref.shape[0]
    chan = wo_ref.shape[0]
    length = tb // SEGS
    dn = pick(mid_ref, t_ref, far_ref).astype(f32)
    x2 = x_ref[...].astype(f32) + rec_ref[...].astype(f32)
    inv = lax.rsqrt(jnp.mean(x2 * x2, axis=-1, keepdims=True) + EPS)
    hat = x2 * inv
    dh = dn * hat
    dg2_ref[...] = jnp.sum(dh, axis=0, keepdims=True)
    g2 = g2_ref[...]
    dot_mean = jnp.mean(dh * g2, axis=-1, keepdims=True)
    dx2 = cot_ref[...].astype(f32) + inv * (dn * g2 - hat * dot_mean)
    dx2_ref[...] = dx2
    drec = dx2.astype(bf16)
    drec_ref[...] = drec
    dgl = dot_nt(drec, wo_ref[...])
    y, slope = gelu_both(ypre_ref[...])
    branch_ref[...] = (dgl * state_ref[...] * slope).astype(bf16)
    dstate = dgl * y
    blocks = chan // 128
    for k in range(blocks):
        ln = slice(k * 128, (k + 1) * 128)
        cbuf[k] = carry_ref[:, ln]
        dbuf[k] = dstate[:, ln]
    ee = [jnp.zeros((SEGS, 128), f32) for _ in range(blocks)]
    qq = [jnp.ones((SEGS, 128), f32) for _ in range(blocks)]
    for j in range(length - 1, -1, -1):
        rows = pl.ds(j, SEGS, stride=length)
        for k in range(blocks):
            a = cbuf[k, rows, :]
            adj = dbuf[k, rows, :] + ee[k]
            al[k, rows, :] = adj
            ql[k, rows, :] = qq[k]
            ee[k] = a * adj
            qq[k] = a * qq[k]
    for k in range(blocks):
        ln = slice(k * 128, (k + 1) * 128)
        qrow = run_ref[0:1, ln]
        erow = run_ref[1:2, ln]
        for s in range(SEGS - 1, -1, -1):
            rows = slice(s * length, (s + 1) * length)
            qseg = ql[k, rows, :]
            adj_ref[rows, ln] = al[k, rows, :] + qseg * erow
            q_ref[rows, ln] = qseg * qrow
            qend = qq[k][s : s + 1, :]
            erow = ee[k][s : s + 1, :] + qend * erow
            qrow = qend * qrow
        end_ref[0:1, ln] = qrow
        end_ref[1:2, ln] = erow


def back_chunk(at, tb, mid, t, far, g2, wo, run, x, rec, cot, state, ypre, carry, carried):
    chan, width = wo.shape
    return chunk_call(
        back_kernel, at, tb, [x, rec, cot, state, ypre, carry], [mid, t, far, g2, wo, run],
        [(width, f32), (width, bf16), (chan, bf16), (chan, f32), (chan, f32)], carried,
        [((2, chan), f32), ((1, width), f32)], 40, "mid_back",
        [pltpu.VMEM((chan // 128, tb, 128), f32)] * 4,
    )


def gates_kernel(
    mine_ref, ends_ref, vec_ref, wai_ref, ue_ref,
    adj_ref, q_ref, a_ref, b_ref, d_ref, g_ref, c_ref, u_ref, before_ref, m_ref, branch_ref,
    du_ref, tail_ref, edge_ref, gw_ref, sums_ref, uext, e1, e2, e3,
):
    tb, chan = adj_ref.shape
    step = pl.program_id(0)
    steps = pl.num_programs(0)
    side = wai_ref.shape[1]
    vec = lambda k: vec_ref[k : k + 1, :]

    @pl.when(step == 0)
    def _():
        for e in (e1, e2, e3):
            e[tb:, :] = jnp.zeros((8, chan), f32)
        gw_ref[...] = jnp.zeros_like(gw_ref)
        sums_ref[...] = jnp.zeros_like(sums_ref)

    @pl.when(step > 0)
    def _():
        for e in (e1, e2, e3):
            e[tb:, :] = e[:8, :]

    uext[HALO:, :] = u_ref[...].astype(f32)

    @pl.when(step == steps - 1)
    def _():
        uext[:HALO, :] = ue_ref[...]

    @pl.when(step < steps - 1)
    def _():
        uext[:HALO, :] = before_ref[...].astype(f32)

    into = entering(ends_ref, mine_ref[0], True)
    keep = m_ref[:, 0:1]
    alive2 = m_ref[:, 1:2]
    alive3 = m_ref[:, 2:3]

    def add(k, ln, value):
        sums_ref[k : k + 1, ln] += jnp.sum(value, axis=0, keepdims=True)

    for k in range(chan // side):
        ln = slice(k * side, (k + 1) * side)
        adj = adj_ref[:, ln] + q_ref[:, ln] * into[:, ln]
        add(2, ln, adj * g_ref[:, ln])
        da = (adj * a_ref[:, ln]).astype(bf16)
        di = (adj * b_ref[:, ln]).astype(bf16)
        add(0, ln, da.astype(f32))
        add(1, ln, di.astype(f32))
        both = jnp.concatenate([da, di], axis=1)
        gw_ref[k] += dot_tn(c_ref[:, ln], both)
        dconv = adj * d_ref[:, ln] + dot_nt(both, wai_ref[k])
        add(3, ln, dconv)
        add(4, ln, dconv * uext[HALO:, ln])
        mk = dconv * keep
        e1[:tb, ln] = mk
        add(5, ln, mk * uext[HALO - 1 : HALO - 1 + tb, ln])
        mk = dconv * alive2
        e2[:tb, ln] = mk
        add(6, ln, mk * uext[HALO - 2 : HALO - 2 + tb, ln])
        mk = dconv * alive3
        e3[:tb, ln] = mk
        add(7, ln, mk * uext[HALO - 3 : HALO - 3 + tb, ln])
        v = lambda j: vec_ref[j : j + 1, ln]
        du = v(2) * dconv + v(3) * e1[1 : 1 + tb, ln]
        du = du + v(4) * e2[2 : 2 + tb, ln] + v(5) * e3[3 : 3 + tb, ln]
        low = du.astype(bf16)
        du_ref[:, ln] = low
        add(8, ln, low.astype(f32))
        add(9, ln, branch_ref[:, ln].astype(f32))

        @pl.when(step == 0)
        def _():
            tail_ref[:, ln] = du[tb - HALO :, :]
            sums_ref[8:9, ln] -= jnp.sum(low[tb - HALO :, :].astype(f32), axis=0, keepdims=True)

    @pl.when(step == steps - 1)
    def _():
        edge_ref[...] = jnp.zeros_like(edge_ref)
        edge_ref[5:6, :] = vec(5) * e3[0:1, :]
        edge_ref[6:7, :] = vec(4) * e2[0:1, :] + vec(5) * e3[1:2, :]
        edge_ref[7:8, :] = vec(3) * e1[0:1, :] + vec(4) * e2[1:2, :] + vec(5) * e3[2:3, :]
        sums_ref[2:3, :] = sums_ref[2:3, :] * vec(10)


def gates_back(mine, ends, vec, wai, ue, adj, q, slope4, c, u, masks, branch, tb):
    rows, chan = adj.shape
    n = rows // tb
    spec = lambda w: pl.BlockSpec((tb, w), lambda b: (n - 1 - b, 0))
    per = tb // HALO
    before = pl.BlockSpec((HALO, chan), lambda b: (jnp.maximum((n - 1 - b) * per - 1, 0), 0))
    blocks, side, two = wai.shape
    return pl.pallas_call(
        gates_kernel,
        grid=(n,),
        in_specs=[SMEM, whole(ends.shape), whole(vec.shape), whole(wai.shape), whole(ue.shape)]
        + [spec(chan)] * 8
        + [before, spec(masks.shape[1]), spec(chan)],
        out_specs=[
            spec(chan), whole((HALO, chan)), whole((8, chan)), whole(wai.shape), whole((16, chan)),
        ],
        out_shape=[
            sds((rows, chan), bf16), sds((HALO, chan), f32), sds((8, chan), f32),
            sds(wai.shape, f32), sds((16, chan), f32),
        ],
        scratch_shapes=[pltpu.VMEM((tb + HALO, chan), f32)] + [pltpu.VMEM((tb + 8, chan), f32)] * 3,
        compiler_params=params(40),
        name="gates_back",
    )(mine, ends, vec, wai, ue, adj, q, *slope4, c, u, u, masks, branch)


def in_kernel(wy_ref, wx_ref, x_ref, branch_ref, du_ref, part_ref, dg1_ref):
    part = dot_nt(branch_ref[...], wy_ref[...]) + dot_nt(du_ref[...], wx_ref[...])
    part_ref[...] = part.astype(bf16)
    x = x_ref[...].astype(f32)
    inv = lax.rsqrt(jnp.mean(x * x, axis=-1, keepdims=True) + EPS)
    dg1_ref[...] = jnp.sum(part * (x * inv), axis=0, keepdims=True)


def in_chunk(at, tb, wy, wx, x, branch, du):
    width = x.shape[1]
    return chunk_call(
        in_kernel, at, tb, [x, branch, du], [wy, wx], [], None,
        [((tb, width), bf16), ((1, width), f32)], 32, "in_back",
    )


def result_kernel(mid_ref, t_ref, far_ref, x_ref, rec_ref, *rest):
    total = x_ref[...].astype(f32) + rec_ref[...].astype(f32)
    rest[-1][...] = (total + pick(mid_ref, t_ref, far_ref).astype(f32)).astype(bf16)


def result_chunk(at, tb, mid, t, far, x, rec, carried):
    return chunk_call(
        result_kernel, at, tb, [x, rec], [mid, t, far], [(x.shape[1], bf16)], carried, [], 24,
        "result",
    )


def last_kernel(mid_ref, t_ref, far_ref, g1_ref, x_ref, dx2_ref, *rest):
    dn = pick(mid_ref, t_ref, far_ref).astype(f32) * g1_ref[...]
    x = x_ref[...].astype(f32)
    inv = lax.rsqrt(jnp.mean(x * x, axis=-1, keepdims=True) + EPS)
    hat = x * inv
    mean = jnp.mean(dn * hat, axis=-1, keepdims=True)
    rest[-1][...] = (dx2_ref[...] + inv * (dn - hat * mean)).astype(bf16)


def last_chunk(at, tb, mid, t, far, g1, x, dx2, carried):
    return chunk_call(
        last_kernel, at, tb, [x, dx2], [mid, t, far, g1], [(x.shape[1], bf16)], carried, [], 24,
        "stream_grad",
    )


def weights_kernel(pairs, offset, *refs):
    out_ref = refs[-1]
    j = pl.program_id(0)
    ins = refs[: 2 * len(pairs)]
    for k in range(len(pairs)):

        @pl.when(j == k)
        def _(k=k):
            at = pl.ds(pl.multiple_of(pl.program_id(1) * out_ref.shape[0], 128), out_ref.shape[0])
            out_ref[...] = dot_tn(ins[2 * k][:, at], ins[2 * k + 1][...]).astype(bf16)


def weights(pairs, db, columns, offset=0, carried=None):
    height = pairs[0][0].shape[1]
    wide = pairs[0][1].shape[1]
    flat = [a for pair in pairs for a in pair]
    once = lambda a: pl.BlockSpec(a.shape, lambda j, i: (0, 0), pipeline_mode=pl.Buffered(1))
    extra = [] if carried is None else [carried]
    return pl.pallas_call(
        functools.partial(weights_kernel, pairs, offset),
        grid=(len(pairs), height // db),
        in_specs=[once(a) for a in flat] + [ANY] * len(extra),
        out_specs=pl.BlockSpec((db, wide), lambda j, i: (i, j + offset)),
        out_shape=sds((height, columns), bf16),
        input_output_aliases={len(flat): 0} if extra else {},
        compiler_params=pltpu.CompilerParams(
            dimension_semantics=("arbitrary", "arbitrary"), vmem_limit_bytes=48 * MIB
        ),
        name="weight_grads",
    )(*flat, *extra)


class Fold:
    def __init__(self, axis):
        self.axis = axis
        self.n = lax.axis_size(axis)
        me = lax.axis_index(axis)
        n = self.n
        self.line = n == 4
        mid = ((me == 1) | (me == 2)) if self.line else me >= 0
        self.mid = mid.astype(jnp.int32)[None]

    def __call__(self, part):
        if not self.line:
            total = lax.psum(part, self.axis)
            return total, total
        got = lax.ppermute(part, self.axis, [(0, 1), (3, 2)])
        s = part + got
        got = lax.ppermute(s, self.axis, [(1, 2), (2, 1)])
        t = s + got
        far = lax.ppermute(t, self.axis, [(1, 0), (2, 3)])
        return t, far


def everyone(value, axis):
    n = lax.axis_size(axis)
    if n & (n - 1):
        return lax.psum(value, axis)
    bit = 1
    while bit < n:
        got = lax.ppermute(value, axis, [(i, i ^ bit) for i in range(n)])
        value = (value.astype(f32) + got.astype(f32)).astype(value.dtype)
        bit *= 2
    return value


def body(
    x, prescale, wy, by, wx, bx, conv_w, conv_b, wa, ba, wi, bi, lam, wo, midscale, wg, wu, wd,
    resets, cot,
):
    rows, width = x.shape
    chan = wy.shape[1]
    hidden = wg.shape[1]
    blocks, side = wa.shape[:2]
    n_seq = lax.axis_size("seq")
    mine = lax.axis_index("seq").astype(jnp.int32)[None]
    fold = Fold("head")
    mid = fold.mid
    tb = 256
    chunks = rows // tb
    order = list(range(chunks - 1, -1, -1))

    g1 = prescale[None]
    g2 = midscale[None]
    keep = 1.0 - resets.astype(f32)
    k1 = jnp.concatenate([jnp.ones((1,), f32), keep[:-1]])
    k2 = jnp.concatenate([jnp.ones((2,), f32), keep[:-2]])
    masks = jnp.stack([keep, keep * k1, keep * k1 * k2, keep], axis=1)
    tail1 = keep[rows - 1]
    tail2 = tail1 * keep[rows - 2]
    zero = jnp.zeros((HALO - 3,), f32)
    edge_mask = jnp.concatenate([zero, jnp.stack([tail2, tail1, jnp.ones((), f32)])])[:, None]
    packed = jnp.concatenate(
        [x[rows - HALO :], jnp.broadcast_to(edge_mask, (HALO, 128)).astype(bf16)], axis=1
    )
    forward = [(i, i + 1) for i in range(n_seq - 1)]
    backward = [(i + 1, i) for i in range(n_seq - 1)]
    xe = lax.ppermute(packed, "seq", forward)
    vec = jnp.concatenate(
        [
            by[None], bx[None], conv_w, conv_b[None], ba[None], bi[None],
            POWER * jax.nn.softplus(-lam)[None], POWER * jax.nn.sigmoid(-lam)[None],
            jnp.zeros((5, chan), f32),
        ],
        axis=0,
    )
    wai = jnp.concatenate([wa, wi], axis=2)

    n1, ypre, u, c, carry, r, i, h, p, end, ue = recur(x, xe, masks, wy, wx, vec, g1, wai, tb)
    ends = lax.all_gather(end, "seq")

    kept = None
    rec_sum = {}
    for at in order:
        *kept, part = out_chunk(at, tb, mine, h, p, ypre, ends, wo, kept)
        rec_sum[at] = fold(part)
    state, gl = kept
    slope4 = slopes(mine, ends, vec, r, i, carry, c, state, masks, tb)

    kept = None
    mlp_part, n2_sum = {}, {}
    for at in order:
        *kept, mlp_part[at], part = mlp_chunk(
            at, tb, mid, *rec_sum[at], g2, wg, wu, wd, x, cot, kept, 384
        )
        n2_sum[at] = fold(part)
    rec, n2, hid, dg, du2 = kept
    big = weights([(n2, dg), (n2, du2), (cot, hid)], 512, 3 * hidden)
    big = lax.psum_scatter(big, "seq", scatter_dimension=0, tiled=True)

    kept = None
    run = jnp.concatenate([jnp.ones((1, chan), f32), jnp.zeros((1, chan), f32)])
    d_g2 = 0.0
    for at in order:
        *kept, run, dg2 = back_chunk(
            at, tb, mid, *n2_sum[at], g2, wo, run, x, rec, cot, state, ypre, carry, kept
        )
        d_g2 = d_g2 + dg2
    dx2, drec, branch, adj, q = kept
    ends_back = lax.all_gather(run, "seq")

    mlp_sum = {at: fold(mlp_part[at]) for at in order}

    du, tail, edge, gw, sums = gates_back(
        mine, ends_back, vec, wai, ue, adj, q, slope4, c, u, masks, branch, tb
    )
    returned = lax.ppermute(edge, "seq", backward)
    patch = tail + jnp.concatenate([jnp.zeros((HALO - 8, chan), f32), returned]) * edge_mask
    patch = patch.astype(bf16)
    du = lax.dynamic_update_slice(du, patch, (rows - HALO, 0))
    sums = sums.at[8].add(jnp.sum(patch.astype(f32), axis=0))

    d_g1 = 0.0
    n1_sum = {}
    for at in range(chunks):
        part, dg1 = in_chunk(at, tb, wy, wx, x, branch, du)
        d_g1 = d_g1 + dg1
        n1_sum[at] = fold(part)
    small = weights([(n1, branch), (n1, du), (drec, gl)], 512, 3 * chan)
    small = lax.psum_scatter(small, "seq", scatter_dimension=0, tiled=True)

    stack = jnp.concatenate([gw.reshape(blocks * side, 2 * side), sums.reshape(-1, 2 * side)])
    stack = everyone(stack.astype(bf16), "seq").astype(f32)
    gw = stack[: blocks * side].reshape(blocks, side, 2 * side)
    sums = stack[blocks * side :].reshape(16, chan)
    gains = jnp.concatenate([d_g1, d_g2 * (1.0 / fold.n)])
    gains = lax.psum(gains, ("seq", "head"))
    piece = width // n_seq
    gains = lax.dynamic_slice(gains, (0, mine[0] * piece), (2, piece))

    result = None
    for at in order:
        result = result_chunk(at, tb, mid, *mlp_sum[at], x, rec, result)
    d_x = None
    for at in range(chunks):
        d_x = last_chunk(at, tb, mid, *n1_sum[at], g1, x, dx2, d_x)

    big = big.astype(f32)
    small = small.astype(f32)
    return (
        result[0], d_x[0], gains[0], small[:, :chan], sums[9], small[:, chan : 2 * chan], sums[8],
        sums[4:8], sums[3], gw[:, :, :side], sums[0], gw[:, :, side:], sums[1], sums[2],
        small[:, 2 * chan :].T, gains[1], big[:, :hidden], big[:, hidden : 2 * hidden],
        big[:, 2 * hidden :].T,
    )


def solution(mesh):
    col, row, both = P(None, "head"), P("head", None), P("seq", "head")
    head, seq, cube = P("head"), P("seq"), P("head", None, None)
    tokens = P("seq", None)
    in_specs = (
        tokens, P(), col, head, col, head, col, head, cube, head, cube, head, head, row, P(), col,
        col, row, seq, tokens,
    )
    out_specs = (
        tokens, tokens, seq, both, head, both, head, col, head, cube, head, cube, head, head,
        P("head", "seq"), seq, both, both, P("head", "seq"),
    )
    return jax.shard_map(body, mesh=mesh, in_specs=in_specs, out_specs=out_specs, check_vma=False)
```

time: 1780 us -> 763 us (0.43)
  local copies, waits for them, and re-layouts: 629 us -> 52.5 us
  waiting for transfers between devices: 651 us -> 332 us
  other arithmetic: 275 us -> 35.4 us
  Pallas kernels: 0 us -> 169 us
  matrix products: 119 us -> 0 us
  starting transfers between devices: 5.42 us -> 84.2 us
    psum x4 -> x0, waiting for transfers between devices: 417 us -> none  [the longest x1 224 us: body(): lax.psum(jnp.dot(hidden, wd, preferred_element_type=f32).astype(jnp.bfloa...]
    ppermute x2 -> x53, waiting for transfers between devices: 0.46 us -> 332 us  [the longest x16 180 us: __call__(): got = lax.ppermute(part, self.axis, [(0, 1), (3, 2)])]
    slice x144 -> x9, local copies, waits for them, and re-layouts: 321 us -> 9.05 us  [the longest x1 2.08 us: body(): small[:, chan:2 * chan]]
    reduce_scatter x6 -> x2, waiting for transfers between devices: 234 us -> 0.01 us  [the longest x1 0.01 us: body(): small = lax.psum_scatter(small, 'seq', scatter_dimension=0, tiled=True)]
    pad x72 -> x0, local copies, waits for them, and re-layouts: 213 us -> none  [the longest x36 107 us: body(): lax.associative_scan(link, (next_carry, d_state), axis=0, reverse=True)]
    pallas_call x0 -> x29, Pallas kernels: none -> 169 us  [the longest x4 55.6 us: mlp_chunk(): pl.pallas_call(mlp_kernel, grid=(hidden // fb,), in_specs=[SMEM, whole(t....]
    dot_general x24 -> x0, matrix products: 119 us -> none  [the longest x1 10.4 us: body(): d_hid = jnp.einsum('td,fd->tf', cotangent, wd, preferred_element_type=f32)]
    ppermute x2 -> x53, starting transfers between devices: 4.44 us -> 84.1 us  [the longest x16 37.2 us: __call__(): got = lax.ppermute(part, self.axis, [(0, 1), (3, 2)])]
  transfers between devices with their start and end apart: 12 -> 55, of which waited for: 10 -> 30; matrix products, arithmetic and copies ran while one was open for 8% -> 6% of each run, Pallas kernels for 0% -> 17%
where the time goes in v1:
time: 763 us; the launch traced here: 753 us
  waiting for transfers between devices  332 us (44%)
  Pallas kernels  169 us (22%)
  starting transfers between devices  84.2 us (11%)
  blocking collectives  62.7 us (8%)
  local copies, waits for them, and re-layouts  52.5 us (7%)
  other arithmetic  35.4 us (5%)
  between operations  17.1 us (2%)
    ppermute x16, waiting for transfers between devices, __call__(): got = lax.ppermute(part, self.axis, [(0, 1), (3, 2)])  180 us
    ppermute x16, waiting for transfers between devices, __call__(): far = lax.ppermute(t, self.axis, [(1, 0), (2, 3)])  149 us
    pallas_call x4, Pallas kernels, mlp_chunk(): pl.pallas_call(mlp_kernel, grid=(hidden // fb,), in_specs=[SMEM, whole(t....  55.6 us
    pallas_call x20, Pallas kernels, chunk_call(): pl.pallas_call(kernel, grid=(1,), in_specs=ins + [spec(a.shape[1]) for a...  49.2 us
    psum x1, blocking collectives, body(): gains = lax.psum(gains, ('seq', 'head'))  43.3 us
    unnamed x140, local copies, waits for them, and re-layouts  40 us
    ppermute x16, starting transfers between devices, __call__(): got = lax.ppermute(part, self.axis, [(0, 1), (3, 2)])  37.2 us
    pallas_call x2, Pallas kernels, weights(): pl.pallas_call(functools.partial(weights_kernel, pairs, offset), grid=(le...  31.6 us
  transfers between devices with their start and end apart: 55, of which 30 were waited for; matrix products, arithmetic and copies ran while one was open for 6% of the time, Pallas kernels for 17%

profile of v1, /device:TPU:0, one launch (start us, length us, event | category | flops | bytes accessed | tf_op | source)
XLA Modules:
  0.0 753.4 jit_solution(14618929509785332626)
XLA Ops:
  11.9 2.3 collective-permute-start
  23.1 17.0 %recur.1 = (bf16[1024,1536]{1,0:T(8,128)(2,1)}, f32[1024,512]{1,0:T(8,128)S(1)}, bf16[1024,512]{1,0:T(8,128)(2,1)S(1)}, bf16[1024,512]{1,0:T(8,128)(2,1)S(1)}, f...) custom-call(bf16[1024,1536]{1,0:T(8,128)(2,1)} %x_ref.41, ...), custom_call_target="tpu_custom_call" | custom-call | tf_op jit(solution)/shard_map/recur/pallas_call | solution.py:159
  43.5 10.1 %all-gather.2.ends_ref = f32[8,2,512]{2,1,0:T(2,128)S(1)} all-gather(f32[1,2,512]{2,1,0:T(2,128)S(1)} %bitcast.44), channel_id=2, replica_groups=mesh['seq'=8,'head'=4] {'seq'}, dimensions={0}, use_global_device_ids=true | all-gather | bytes 36864 | tf_op jit(solution)/shard_map/all_gather | solution.py:696
  57.5 3.5 collective-permute-start.10
  67.2 11.6 %collective-permute-done.10 = bf16[256,1536]{1,0:T(8,128)(2,1)S(1)} collective-permute-done((bf16[256,1536]{1,0:T(8,128)(2,1)S(1)}, bf16[256,1536]{1,0:T(8,128)(2,1)S(1)}, u32[]{:S(2)}, u32[]{:S(2)}) %collective-permute-start.10) | collective-permute-done | bytes 786464 | tf_op jit(solution)/shard_map/ppermute | solution.py:633
  79.8 15.9 %collective-permute-done.7 = bf16[256,1536]{1,0:T(8,128)(2,1)S(1)} collective-permute-done((bf16[256,1536]{1,0:T(8,128)(2,1)S(1)}, bf16[256,1536]{1,0:T(8,128)(2,1)S(1)}, u32[]{:S(2)}, u32[]{:S(2)}) %collective-permute-start.7) | collective-permute-done | bytes 786464 | tf_op jit(solution)/shard_map/ppermute | solution.py:633
  96.6 15.9 %collective-permute-done.4 = bf16[256,1536]{1,0:T(8,128)(2,1)S(1)} collective-permute-done((bf16[256,1536]{1,0:T(8,128)(2,1)S(1)}, bf16[256,1536]{1,0:T(8,128)(2,1)S(1)}, u32[]{:S(2)}, u32[]{:S(2)}) %collective-permute-start.4) | collective-permute-done | bytes 786464 | tf_op jit(solution)/shard_map/ppermute | solution.py:633
  113.5 15.4 %collective-permute-done.1 = bf16[256,1536]{1,0:T(8,128)(2,1)S(1)} collective-permute-done((bf16[256,1536]{1,0:T(8,128)(2,1)S(1)}, bf16[256,1536]{1,0:T(8,128)(2,1)S(1)}, u32[]{:S(2)}, u32[]{:S(2)}) %collective-permute-start.1) | collective-permute-done | bytes 786464 | tf_op jit(solution)/shard_map/ppermute | solution.py:633
  139.6 16.5 %collective-permute-done.12.far_ref = bf16[256,1536]{1,0:T(8,128)(2,1)} collective-permute-done((bf16[256,1536]{1,0:T(8,128)(2,1)}, bf16[256,1536]{1,0:T(8,128)(2,1)}, u32[]{:S(2)}, u32[]{:S(2)}) %collective-permute-start.12) | collective-permute-done | bytes 786464 | tf_op jit(solution)/shard_map/ppermute | solution.py:637
  156.1 13.9 %mlp.4 = (bf16[1024,1536]{1,0:T(8,128)(2,1)S(1)}, bf16[1024,1536]{1,0:T(8,128)(2,1)}, bf16[1024,1152]{1,0:T(8,128)(2,1)S(1)}, bf16[1024,1152]{1,0:T(8,128)(2,1)S...) custom-call(s32[1]{0:T(128)} %bitcast.mid_ref, ...), custom_call_target="tpu_custom_call" | custom-call | tf_op jit(solution)/shard_map/mlp/pallas_call | solution.py:344
  173.0 13.9 %mlp.5 = (bf16[1024,1536]{1,0:T(8,128)(2,1)S(1)}, bf16[1024,1536]{1,0:T(8,128)(2,1)}, bf16[1024,1152]{1,0:T(8,128)(2,1)S(1)}, bf16[1024,1152]{1,0:T(8,128)(2,1)S...) custom-call(s32[1]{0:T(128)} %bitcast.mid_ref, ...), custom_call_target="tpu_custom_call", output_to_operand_aliasing={{0}: (9, {}), {1}: (10, {}), {2}: (11, {}), {3}: (12, {}), ... | custom-call | tf_op jit(solution)/shard_map/mlp/pallas_call | solution.py:344
  189.8 13.9 %mlp.6 = (bf16[1024,1536]{1,0:T(8,128)(2,1)S(1)}, bf16[1024,1536]{1,0:T(8,128)(2,1)}, bf16[1024,1152]{1,0:T(8,128)(2,1)S(1)}, bf16[1024,1152]{1,0:T(8,128)(2,1)S...) custom-call(s32[1]{0:T(128)} %bitcast.mid_ref, ...), custom_call_target="tpu_custom_call", output_to_operand_aliasing={{0}: (9, {}), {1}: (10, {}), {2}: (11, {}), {3}: (12, {}), ... | custom-call | tf_op jit(solution)/shard_map/mlp/pallas_call | solution.py:344
  204.6 1.9 collective-permute-start.28
  206.5 13.9 %mlp.7 = (bf16[1024,1536]{1,0:T(8,128)(2,1)S(1)}, bf16[1024,1536]{1,0:T(8,128)(2,1)}, bf16[1024,1152]{1,0:T(8,128)(2,1)S(1)}, bf16[1024,1152]{1,0:T(8,128)(2,1)S...) custom-call(s32[1]{0:T(128)} %bitcast.mid_ref, ...), custom_call_target="tpu_custom_call", output_to_operand_aliasing={{0}: (9, {}), {1}: (10, {}), {2}: (11, {}), {3}: (12, {}), ... | custom-call | tf_op jit(solution)/shard_map/mlp/pallas_call | solution.py:344
  228.9 11.6 %collective-permute-done.25 = bf16[256,1536]{1,0:T(8,128)(2,1)S(1)} collective-permute-done((bf16[256,1536]{1,0:T(8,128)(2,1)S(1)}, bf16[256,1536]{1,0:T(8,128)(2,1)S(1)}, u32[]{:S(2)}, u32[]{:S(2)}) %collective-permute-start.25) | collective-permute-done | bytes 786464 | tf_op jit(solution)/shard_map/ppermute | solution.py:633
  248.0 7.4 slopes.1
  258.1 4.3 collective-permute-done.36.far_ref
  262.4 4.9 mid_back.4
  267.3 12.3 %collective-permute-done.33.far_ref = bf16[256,1536]{1,0:T(8,128)(2,1)} collective-permute-done((bf16[256,1536]{1,0:T(8,128)(2,1)S(1)}, bf16[256,1536]{1,0:T(8,128)(2,1)}, u32[]{:S(2)}, u32[]{:S(2)}) %collective-permute-start.33) | collective-permute-done | bytes 786464 | tf_op jit(solution)/shard_map/ppermute | solution.py:637
  279.7 5.1 mid_back.5
  284.8 11.6 %collective-permute-done.30.far_ref = bf16[256,1536]{1,0:T(8,128)(2,1)S(1)} collective-permute-done((bf16[256,1536]{1,0:T(8,128)(2,1)S(1)}, bf16[256,1536]{1,0:T(8,128)(2,1)S(1)}, u32[]{:S(2)}, u32[]{:S(2)}) %collective-permute-start.30) | collective-permute-done | bytes 786464 | tf_op jit(solution)/shard_map/ppermute | solution.py:637
  296.4 4.9 mid_back.6
  301.4 10.6 %collective-permute-done.27.far_ref = bf16[256,1536]{1,0:T(8,128)(2,1)S(1)} collective-permute-done((bf16[256,1536]{1,0:T(8,128)(2,1)S(1)}, bf16[256,1536]{1,0:T(8,128)(2,1)S(1)}, u32[]{:S(2)}, u32[]{:S(2)}) %collective-permute-start.27) | collective-permute-done | bytes 786464 | tf_op jit(solution)/shard_map/ppermute | solution.py:637
  312.0 5.0 mid_back.7
  317.0 9.3 %all-gather.3.ends_ref = f32[8,2,512]{2,1,0:T(2,128)S(1)} all-gather(f32[1,2,512]{2,1,0:T(2,128)S(1)} %bitcast.43), channel_id=3, replica_groups=mesh['seq'=8,'head'=4] {'seq'}, dimensions={0}, use_global_device_ids=true | all-gather | bytes 36864 | tf_op jit(solution)/shard_map/all_gather | solution.py:726
  327.9 8.6 %gates_back.1 = (bf16[1024,512]{1,0:T(8,128)(2,1)S(1)}, f32[16,512]{1,0:T(8,128)S(1)}, f32[8,512]{1,0:T(8,128)S(1)}, f32[4,128,256]{2,1,0:T(8,128)S(1)}, f32[16,512]{1,0:T(8,128)S(1)}) custom-call(s32[1]{0:T(128)} %bitcast.1.mine_ref, f32[8,2,512]{2,1,0:T(2,128)S(1)} %all-gather.3.ends_ref, f32[16,512]{1,0:T(8,128)S(1)} %concatenate.34.vec_ref, ...), custom_call_target="tpu_custom_call" | custom-call | tf_op jit(solution)/shard_map/gates_back/pallas_call | solution.py:524
  340.5 11.8 %weight_grads.2 = bf16[1536,1536]{1,0:T(8,128)(2,1)} custom-call(bf16[1024,1536]{1,0:T(8,128)(2,1)} %get-tuple-element.214.refs_0_.refs_2_, bf16[1024,512]{1,0:T(8,128)(2,1)S(1)} %get-tuple-element.185.branch_ref.refs_1_, bf16[1024,1536]{1,0:T(8,128)(2,1)} %get-tuple-element.214.refs_0_.refs_2_, ...), custom_call_target="tpu_custom_call" | custom-call | tf_op jit(solution)/shard_map/weight_grads/pallas_call | solution.py:605
  356.6 19.8 %weight_grads.3 = bf16[1536,3456]{1,0:T(8,128)(2,1)} custom-call(bf16[1024,1536]{1,0:T(8,128)(2,1)} %get-tuple-element.219.refs_0_.refs_2_, bf16[1024,1152]{1,0:T(8,128)(2,1)S(1)} %copy-done.18, bf16[1024,1536]{1,0:T(8,128)(2,1)} %get-tuple-element.219.refs_0_.refs_2_, bf16[1024,1152]{1,0:T(8,128)(2,1)S(1)} %copy-done.20, bf16[1024,1536]{1,0:T(8,128)(2,1)} %refs_4_.1, ...), custom_call_target="tpu_custom_call" | custom-call | tf_op jit(solution)/shard_map/weight_grads/pallas_call | solution.py:605
  377.6 13.6 %collective-permute-start.22 = (bf16[256,1536]{1,0:T(8,128)(2,1)S(1)}, bf16[256,1536]{1,0:T(8,128)(2,1)S(1)}, u32[]{:S(2)}, u32[]{:S(2)}) collective-permute-start(bf16[256,1536]{1,0:T(8,128)(2,1)S(1)} %copy-done.40), channel_id=1, source_target_pairs={{0,1},{3,2},{4,5},{7,6},{8,9},{11,10},{12,13},{15,14},{16,17},{19,... | collective-permute-start | bytes 2359304 | tf_op jit(solution)/shard_map/ppermute | solution.py:633
  395.2 12.0 %collective-permute-done.22 = bf16[256,1536]{1,0:T(8,128)(2,1)S(1)} collective-permute-done((bf16[256,1536]{1,0:T(8,128)(2,1)S(1)}, bf16[256,1536]{1,0:T(8,128)(2,1)S(1)}, u32[]{:S(2)}, u32[]{:S(2)}) %collective-permute-start.22) | collective-permute-done | bytes 786464 | tf_op jit(solution)/shard_map/ppermute | solution.py:633
  408.2 15.9 %collective-permute-done.19 = bf16[256,1536]{1,0:T(8,128)(2,1)S(1)} collective-permute-done((bf16[256,1536]{1,0:T(8,128)(2,1)S(1)}, bf16[256,1536]{1,0:T(8,128)(2,1)S(1)}, u32[]{:S(2)}, u32[]{:S(2)}) %collective-permute-start.19) | collective-permute-done | bytes 786464 | tf_op jit(solution)/shard_map/ppermute | solution.py:633
  425.0 15.9 %collective-permute-done.16 = bf16[256,1536]{1,0:T(8,128)(2,1)S(1)} collective-permute-done((bf16[256,1536]{1,0:T(8,128)(2,1)S(1)}, bf16[256,1536]{1,0:T(8,128)(2,1)S(1)}, u32[]{:S(2)}, u32[]{:S(2)}) %collective-permute-start.16) | collective-permute-done | bytes 786464 | tf_op jit(solution)/shard_map/ppermute | solution.py:633
  441.9 15.9 %collective-permute-done.13 = bf16[256,1536]{1,0:T(8,128)(2,1)S(1)} collective-permute-done((bf16[256,1536]{1,0:T(8,128)(2,1)S(1)}, bf16[256,1536]{1,0:T(8,128)(2,1)S(1)}, u32[]{:S(2)}, u32[]{:S(2)}) %collective-permute-start.13) | collective-permute-done | bytes 786464 | tf_op jit(solution)/shard_map/ppermute | solution.py:633
  469.8 13.6 %collective-permute-done.24.far_ref = bf16[256,1536]{1,0:T(8,128)(2,1)} collective-permute-done((bf16[256,1536]{1,0:T(8,128)(2,1)}, bf16[256,1536]{1,0:T(8,128)(2,1)}, u32[]{:S(2)}, u32[]{:S(2)}) %collective-permute-start.24) | collective-permute-done | bytes 786464 | tf_op jit(solution)/shard_map/ppermute | solution.py:637
  483.4 2.1 copy-done.2
  485.6 2.6 result.4.rest_0_
  488.2 12.1 %collective-permute-done.21.far_ref = bf16[256,1536]{1,0:T(8,128)(2,1)} collective-permute-done((bf16[256,1536]{1,0:T(8,128)(2,1)}, bf16[256,1536]{1,0:T(8,128)(2,1)}, u32[]{:S(2)}, u32[]{:S(2)}) %collective-permute-start.21) | collective-permute-done | bytes 786464 | tf_op jit(solution)/shard_map/ppermute | solution.py:637
  500.3 2.6 result.5.rest_0_
  502.9 14.3 %collective-permute-done.18.far_ref = bf16[256,1536]{1,0:T(8,128)(2,1)} collective-permute-done((bf16[256,1536]{1,0:T(8,128)(2,1)}, bf16[256,1536]{1,0:T(8,128)(2,1)}, u32[]{:S(2)}, u32[]{:S(2)}) %collective-permute-start.18) | collective-permute-done | bytes 786464 | tf_op jit(solution)/shard_map/ppermute | solution.py:637
  517.2 2.6 result.6.rest_0_
  519.7 14.3 %collective-permute-done.15.far_ref = bf16[256,1536]{1,0:T(8,128)(2,1)} collective-permute-done((bf16[256,1536]{1,0:T(8,128)(2,1)}, bf16[256,1536]{1,0:T(8,128)(2,1)}, u32[]{:S(2)}, u32[]{:S(2)}) %collective-permute-start.15) | collective-permute-done | bytes 786464 | tf_op jit(solution)/shard_map/ppermute | solution.py:637
  534.0 2.6 result.7
  552.1 3.4 collective-permute-start.51
  555.6 8.6 %collective-permute-done.47 = bf16[256,1536]{1,0:T(8,128)(2,1)S(1)} collective-permute-done((bf16[256,1536]{1,0:T(8,128)(2,1)}, bf16[256,1536]{1,0:T(8,128)(2,1)S(1)}, u32[]{:S(2)}, u32[]{:S(2)}) %collective-permute-start.47) | collective-permute-done | bytes 786464 | tf_op jit(solution)/shard_map/ppermute | solution.py:633
  564.1 2.2 add.186
  568.1 12.9 %collective-permute-done.44 = bf16[256,1536]{1,0:T(8,128)(2,1)S(1)} collective-permute-done((bf16[256,1536]{1,0:T(8,128)(2,1)}, bf16[256,1536]{1,0:T(8,128)(2,1)S(1)}, u32[]{:S(2)}, u32[]{:S(2)}) %collective-permute-start.44) | collective-permute-done | bytes 786464 | tf_op jit(solution)/shard_map/ppermute | solution.py:633
  583.7 14.2 %collective-permute-done.41 = bf16[256,1536]{1,0:T(8,128)(2,1)S(1)} collective-permute-done((bf16[256,1536]{1,0:T(8,128)(2,1)}, bf16[256,1536]{1,0:T(8,128)(2,1)S(1)}, u32[]{:S(2)}, u32[]{:S(2)}) %collective-permute-start.41) | collective-permute-done | bytes 786464 | tf_op jit(solution)/shard_map/ppermute | solution.py:633
  600.4 14.2 %collective-permute-done.38 = bf16[256,1536]{1,0:T(8,128)(2,1)S(1)} collective-permute-done((bf16[256,1536]{1,0:T(8,128)(2,1)}, bf16[256,1536]{1,0:T(8,128)(2,1)S(1)}, u32[]{:S(2)}, u32[]{:S(2)}) %collective-permute-start.38) | collective-permute-done | bytes 786464 | tf_op jit(solution)/shard_map/ppermute | solution.py:633
  617.4 2.0 collective-permute-start.52
  619.4 43.3 %psum.7 = f32[2,1536]{1,0:T(2,128)S(1)} all-reduce(f32[2,1536]{1,0:T(2,128)S(1)} %pad_maximum_fusion.3), channel_id=1, replica_groups=mesh['seq'=8,'head'=4] {'seq','head'}, use_global_device_ids=true, to_apply=%region_0.1 | all-reduce | flops 3072 | bytes 24576 | tf_op jit(solution)/shard_map/psum | solution.py:753
  662.8 2.4 add.187.t_ref
  666.5 2.4 add.185.t_ref
  670.3 2.4 add.183.t_ref
  674.0 2.4 add.181.t_ref
  685.6 1.9 fusion.5
  687.9 2.8 copy-done.3
  690.7 3.0 stream_grad.4.rest_0_
  693.7 11.0 %collective-permute-done.46.far_ref = bf16[256,1536]{1,0:T(8,128)(2,1)} collective-permute-done((bf16[256,1536]{1,0:T(8,128)(2,1)}, bf16[256,1536]{1,0:T(8,128)(2,1)}, u32[]{:S(2)}, u32[]{:S(2)}) %collective-permute-start.46) | collective-permute-done | bytes 786464 | tf_op jit(solution)/shard_map/ppermute | solution.py:637
  704.8 3.0 stream_grad.5.rest_0_
  707.8 13.8 %collective-permute-done.43.far_ref = bf16[256,1536]{1,0:T(8,128)(2,1)} collective-permute-done((bf16[256,1536]{1,0:T(8,128)(2,1)}, bf16[256,1536]{1,0:T(8,128)(2,1)}, u32[]{:S(2)}, u32[]{:S(2)}) %collective-permute-start.43) | collective-permute-done | bytes 786464 | tf_op jit(solution)/shard_map/ppermute | solution.py:637
  721.6 3.0 stream_grad.6.rest_0_
  724.6 11.8 %collective-permute-done.40.far_ref = bf16[256,1536]{1,0:T(8,128)(2,1)} collective-permute-done((bf16[256,1536]{1,0:T(8,128)(2,1)}, bf16[256,1536]{1,0:T(8,128)(2,1)}, u32[]{:S(2)}, u32[]{:S(2)}) %collective-permute-start.40) | collective-permute-done | bytes 786464 | tf_op jit(solution)/shard_map/ppermute | solution.py:637
  736.5 3.0 stream_grad.7
  740.7 2.1 fusion.4
  (291 shorter events, 136.7 us)
Async XLA Ops:
  7.2 732.3 %reduce-scatter.3.cloned.1.call-start = ((), (), s32[]{:S(2)}) async-start(), calls=%async_computation.2 | async-start | bytes 5308416 | tf_op jit(solution)/shard_map/reduce_scatter | solution.py:746
  11.9 8.2 %collective-permute-start = (bf16[16,1664]{1,0:T(8,128)(2,1)S(1)}, bf16[16,1664]{1,0:T(8,128)(2,1)S(1)}, u32[]{:S(2)}, u32[]{:S(2)}) collective-permute-start(bf16[16,1664]{1,0:T(8,128)(2,1)S(1)} %pad_maximum_fusion.1), channel_id=1, source_target_pairs={{0,4},{4,8},{8,12},{12,16},{16,20},{20,24},{24,28},{1,5},{5,9},{9,... | collective-permute-start | bytes 159752 | tf_op jit(solution)/shard_map/ppermute | solution.py:684
  17.9 22.2 %copy-start.25 = (f32[1024,4]{1,0:T(8,128)}, f32[1024,4]{1,0:T(8,128)S(1)}, u32[]{:S(2)}) copy-start(f32[1024,4]{1,0:T(8,128)S(1)} %copy.85.m_ref) | copy-start | bytes 49156
  20.1 33.5 %copy-start.6 = (bf16[512,1536]{1,0:T(8,128)(2,1)S(1)}, bf16[512,1536]{1,0:T(8,128)(2,1)}, u32[]{:S(2)}) copy-start(bf16[512,1536]{1,0:T(8,128)(2,1)} %wo_ref.15) | copy-start | bytes 4718596
  43.5 21.6 %copy-start.4 = (f32[1024,512]{1,0:T(8,128)}, f32[1024,512]{1,0:T(8,128)S(1)}, u32[]{:S(2)}) copy-start(f32[1024,512]{1,0:T(8,128)S(1)} %get-tuple-element.130.ypre_ref) | copy-start | bytes 6291460
  57.5 21.4 %collective-permute-start.10 = (bf16[256,1536]{1,0:T(8,128)(2,1)S(1)}, bf16[256,1536]{1,0:T(8,128)(2,1)S(1)}, u32[]{:S(2)}, u32[]{:S(2)}) collective-permute-start(bf16[256,1536]{1,0:T(8,128)(2,1)S(1)} %get-tuple-element.140), channel_id=1, source_target_pairs={{0,1},{3,2},{4,5},{7,6},{8,9},{11,10},{12,13},{15,14},{16,17},{19,... | collective-permute-start | bytes 2359304 | tf_op jit(solution)/shard_map/ppermute | solution.py:633
  61.7 34.0 %collective-permute-start.7 = (bf16[256,1536]{1,0:T(8,128)(2,1)S(1)}, bf16[256,1536]{1,0:T(8,128)(2,1)S(1)}, u32[]{:S(2)}, u32[]{:S(2)}) collective-permute-start(bf16[256,1536]{1,0:T(8,128)(2,1)S(1)} %get-tuple-element.139), channel_id=1, source_target_pairs={{0,1},{3,2},{4,5},{7,6},{8,9},{11,10},{12,13},{15,14},{16,17},{19,... | collective-permute-start | bytes 2359304 | tf_op jit(solution)/shard_map/ppermute | solution.py:633
  63.8 48.7 %collective-permute-start.4 = (bf16[256,1536]{1,0:T(8,128)(2,1)S(1)}, bf16[256,1536]{1,0:T(8,128)(2,1)S(1)}, u32[]{:S(2)}, u32[]{:S(2)}) collective-permute-start(bf16[256,1536]{1,0:T(8,128)(2,1)S(1)} %get-tuple-element.138), channel_id=1, source_target_pairs={{0,1},{3,2},{4,5},{7,6},{8,9},{11,10},{12,13},{15,14},{16,17},{19,... | collective-permute-start | bytes 2359304 | tf_op jit(solution)/shard_map/ppermute | solution.py:633
  65.9 62.9 %collective-permute-start.1 = (bf16[256,1536]{1,0:T(8,128)(2,1)S(1)}, bf16[256,1536]{1,0:T(8,128)(2,1)S(1)}, u32[]{:S(2)}, u32[]{:S(2)}) collective-permute-start(bf16[256,1536]{1,0:T(8,128)(2,1)S(1)} %get-tuple-element.137), channel_id=1, source_target_pairs={{0,1},{3,2},{4,5},{7,6},{8,9},{11,10},{12,13},{15,14},{16,17},{19,... | collective-permute-start | bytes 2359304 | tf_op jit(solution)/shard_map/ppermute | solution.py:633
  79.0 50.7 %collective-permute-start.11 = (bf16[256,1536]{1,0:T(8,128)(2,1)S(1)}, bf16[256,1536]{1,0:T(8,128)(2,1)S(1)}, u32[]{:S(2)}, u32[]{:S(2)}) collective-permute-start(bf16[256,1536]{1,0:T(8,128)(2,1)S(1)} %add.161), channel_id=1, source_target_pairs={{1,2},{2,1},{5,6},{6,5},{9,10},{10,9},{13,14},{14,13},{17,18},{18,... | collective-permute-start | bytes 2359304 | tf_op jit(solution)/shard_map/ppermute | solution.py:635
  95.9 36.2 %collective-permute-start.8 = (bf16[256,1536]{1,0:T(8,128)(2,1)S(1)}, bf16[256,1536]{1,0:T(8,128)(2,1)S(1)}, u32[]{:S(2)}, u32[]{:S(2)}) collective-permute-start(bf16[256,1536]{1,0:T(8,128)(2,1)S(1)} %add.159), channel_id=1, source_target_pairs={{1,2},{2,1},{5,6},{6,5},{9,10},{10,9},{13,14},{14,13},{17,18},{18,... | collective-permute-start | bytes 2359304 | tf_op jit(solution)/shard_map/ppermute | solution.py:635
  112.7 21.9 %collective-permute-start.5 = (bf16[256,1536]{1,0:T(8,128)(2,1)S(1)}, bf16[256,1536]{1,0:T(8,128)(2,1)S(1)}, u32[]{:S(2)}, u32[]{:S(2)}) collective-permute-start(bf16[256,1536]{1,0:T(8,128)(2,1)S(1)} %add.157), channel_id=1, source_target_pairs={{1,2},{2,1},{5,6},{6,5},{9,10},{10,9},{13,14},{14,13},{17,18},{18,... | collective-permute-start | bytes 2359304 | tf_op jit(solution)/shard_map/ppermute | solution.py:635
  129.0 8.0 %collective-permute-start.2 = (bf16[256,1536]{1,0:T(8,128)(2,1)S(1)}, bf16[256,1536]{1,0:T(8,128)(2,1)S(1)}, u32[]{:S(2)}, u32[]{:S(2)}) collective-permute-start(bf16[256,1536]{1,0:T(8,128)(2,1)S(1)} %add.155), channel_id=1, source_target_pairs={{1,2},{2,1},{5,6},{6,5},{9,10},{10,9},{13,14},{14,13},{17,18},{18,... | collective-permute-start | bytes 2359304 | tf_op jit(solution)/shard_map/ppermute | solution.py:635
  130.8 25.3 %collective-permute-start.12 = (bf16[256,1536]{1,0:T(8,128)(2,1)}, bf16[256,1536]{1,0:T(8,128)(2,1)}, u32[]{:S(2)}, u32[]{:S(2)}) collective-permute-start(bf16[256,1536]{1,0:T(8,128)(2,1)} %add.162.t_ref), channel_id=1, source_target_pairs={{1,0},{2,3},{5,4},{6,7},{9,8},{10,11},{13,12},{14,15},{17,16},{18,... | collective-permute-start | bytes 2359304 | tf_op jit(solution)/shard_map/ppermute | solution.py:637
  133.2 39.8 %collective-permute-start.9 = (bf16[256,1536]{1,0:T(8,128)(2,1)}, bf16[256,1536]{1,0:T(8,128)(2,1)}, u32[]{:S(2)}, u32[]{:S(2)}) collective-permute-start(bf16[256,1536]{1,0:T(8,128)(2,1)} %add.160.t_ref), channel_id=1, source_target_pairs={{1,0},{2,3},{5,4},{6,7},{9,8},{10,11},{13,12},{14,15},{17,16},{18,... | collective-permute-start | bytes 2359304 | tf_op jit(solution)/shard_map/ppermute | solution.py:637
  135.7 54.1 %collective-permute-start.6 = (bf16[256,1536]{1,0:T(8,128)(2,1)}, bf16[256,1536]{1,0:T(8,128)(2,1)}, u32[]{:S(2)}, u32[]{:S(2)}) collective-permute-start(bf16[256,1536]{1,0:T(8,128)(2,1)} %add.158.t_ref), channel_id=1, source_target_pairs={{1,0},{2,3},{5,4},{6,7},{9,8},{10,11},{13,12},{14,15},{17,16},{18,... | collective-permute-start | bytes 2359304 | tf_op jit(solution)/shard_map/ppermute | solution.py:637
  138.1 68.4 %collective-permute-start.3 = (bf16[256,1536]{1,0:T(8,128)(2,1)}, bf16[256,1536]{1,0:T(8,128)(2,1)}, u32[]{:S(2)}, u32[]{:S(2)}) collective-permute-start(bf16[256,1536]{1,0:T(8,128)(2,1)} %add.156.t_ref), channel_id=1, source_target_pairs={{1,0},{2,3},{5,4},{6,7},{9,8},{10,11},{13,12},{14,15},{17,16},{18,... | collective-permute-start | bytes 2359304 | tf_op jit(solution)/shard_map/ppermute | solution.py:637
  170.0 56.1 %collective-permute-start.34 = (bf16[256,1536]{1,0:T(8,128)(2,1)S(1)}, bf16[256,1536]{1,0:T(8,128)(2,1)S(1)}, u32[]{:S(2)}, u32[]{:S(2)}) collective-permute-start(bf16[256,1536]{1,0:T(8,128)(2,1)S(1)} %get-tuple-element.164), channel_id=1, source_target_pairs={{0,1},{3,2},{4,5},{7,6},{8,9},{11,10},{12,13},{15,14},{16,17},{19,... | collective-permute-start | bytes 2359304 | tf_op jit(solution)/shard_map/ppermute | solution.py:633
  187.7 39.3 %collective-permute-start.31 = (bf16[256,1536]{1,0:T(8,128)(2,1)S(1)}, bf16[256,1536]{1,0:T(8,128)(2,1)S(1)}, u32[]{:S(2)}, u32[]{:S(2)}) collective-permute-start(bf16[256,1536]{1,0:T(8,128)(2,1)S(1)} %get-tuple-element.163), channel_id=1, source_target_pairs={{0,1},{3,2},{4,5},{7,6},{8,9},{11,10},{12,13},{15,14},{16,17},{19,... | collective-permute-start | bytes 2359304 | tf_op jit(solution)/shard_map/ppermute | solution.py:633
  204.6 23.4 %collective-permute-start.28 = (bf16[256,1536]{1,0:T(8,128)(2,1)S(1)}, bf16[256,1536]{1,0:T(8,128)(2,1)S(1)}, u32[]{:S(2)}, u32[]{:S(2)}) collective-permute-start(bf16[256,1536]{1,0:T(8,128)(2,1)S(1)} %get-tuple-element.162), channel_id=1, source_target_pairs={{0,1},{3,2},{4,5},{7,6},{8,9},{11,10},{12,13},{15,14},{16,17},{19,... | collective-permute-start | bytes 2359304 | tf_op jit(solution)/shard_map/ppermute | solution.py:633
  224.8 15.8 %collective-permute-start.25 = (bf16[256,1536]{1,0:T(8,128)(2,1)S(1)}, bf16[256,1536]{1,0:T(8,128)(2,1)S(1)}, u32[]{:S(2)}, u32[]{:S(2)}) collective-permute-start(bf16[256,1536]{1,0:T(8,128)(2,1)S(1)} %get-tuple-element.161), channel_id=1, source_target_pairs={{0,1},{3,2},{4,5},{7,6},{8,9},{11,10},{12,13},{15,14},{16,17},{19,... | collective-permute-start | bytes 2359304 | tf_op jit(solution)/shard_map/ppermute | solution.py:633
  226.3 15.1 %collective-permute-start.35 = (bf16[256,1536]{1,0:T(8,128)(2,1)S(1)}, bf16[256,1536]{1,0:T(8,128)(2,1)S(1)}, u32[]{:S(2)}, u32[]{:S(2)}) collective-permute-start(bf16[256,1536]{1,0:T(8,128)(2,1)S(1)} %add.177), channel_id=1, source_target_pairs={{1,2},{2,1},{5,6},{6,5},{9,10},{10,9},{13,14},{14,13},{17,18},{18,... | collective-permute-start | bytes 2359304 | tf_op jit(solution)/shard_map/ppermute | solution.py:635
  227.3 15.8 %collective-permute-start.32 = (bf16[256,1536]{1,0:T(8,128)(2,1)S(1)}, bf16[256,1536]{1,0:T(8,128)(2,1)S(1)}, u32[]{:S(2)}, u32[]{:S(2)}) collective-permute-start(bf16[256,1536]{1,0:T(8,128)(2,1)S(1)} %add.175), channel_id=1, source_target_pairs={{1,2},{2,1},{5,6},{6,5},{9,10},{10,9},{13,14},{14,13},{17,18},{18,... | collective-permute-start | bytes 2359304 | tf_op jit(solution)/shard_map/ppermute | solution.py:635
  228.2 16.7 %collective-permute-start.29 = (bf16[256,1536]{1,0:T(8,128)(2,1)S(1)}, bf16[256,1536]{1,0:T(8,128)(2,1)S(1)}, u32[]{:S(2)}, u32[]{:S(2)}) collective-permute-start(bf16[256,1536]{1,0:T(8,128)(2,1)S(1)} %add.173), channel_id=1, source_target_pairs={{1,2},{2,1},{5,6},{6,5},{9,10},{10,9},{13,14},{14,13},{17,18},{18,... | collective-permute-start | bytes 2359304 | tf_op jit(solution)/shard_map/ppermute | solution.py:635
  240.7 5.7 collective-permute-start.26
  241.7 20.7 %collective-permute-start.36 = (bf16[256,1536]{1,0:T(8,128)(2,1)S(1)}, bf16[256,1536]{1,0:T(8,128)(2,1)S(1)}, u32[]{:S(2)}, u32[]{:S(2)}) collective-permute-start(bf16[256,1536]{1,0:T(8,128)(2,1)S(1)} %add.178.t_ref), channel_id=1, source_target_pairs={{1,0},{2,3},{5,4},{6,7},{9,8},{10,11},{13,12},{14,15},{17,16},{18,... | collective-permute-start | bytes 2359304 | tf_op jit(solution)/shard_map/ppermute | solution.py:637
  243.3 36.3 %collective-permute-start.33 = (bf16[256,1536]{1,0:T(8,128)(2,1)S(1)}, bf16[256,1536]{1,0:T(8,128)(2,1)}, u32[]{:S(2)}, u32[]{:S(2)}) collective-permute-start(bf16[256,1536]{1,0:T(8,128)(2,1)S(1)} %add.176.t_ref), channel_id=1, source_target_pairs={{1,0},{2,3},{5,4},{6,7},{9,8},{10,11},{13,12},{14,15},{17,16},{18,... | collective-permute-start | bytes 2359304 | tf_op jit(solution)/shard_map/ppermute | solution.py:637
  245.1 51.3 %collective-permute-start.30 = (bf16[256,1536]{1,0:T(8,128)(2,1)S(1)}, bf16[256,1536]{1,0:T(8,128)(2,1)S(1)}, u32[]{:S(2)}, u32[]{:S(2)}) collective-permute-start(bf16[256,1536]{1,0:T(8,128)(2,1)S(1)} %add.174.t_ref), channel_id=1, source_target_pairs={{1,0},{2,3},{5,4},{6,7},{9,8},{10,11},{13,12},{14,15},{17,16},{18,... | collective-permute-start | bytes 2359304 | tf_op jit(solution)/shard_map/ppermute | solution.py:637
  246.6 65.4 %collective-permute-start.27 = (bf16[256,1536]{1,0:T(8,128)(2,1)S(1)}, bf16[256,1536]{1,0:T(8,128)(2,1)S(1)}, u32[]{:S(2)}, u32[]{:S(2)}) collective-permute-start(bf16[256,1536]{1,0:T(8,128)(2,1)S(1)} %add.172.t_ref), channel_id=1, source_target_pairs={{1,0},{2,3},{5,4},{6,7},{9,8},{10,11},{13,12},{14,15},{17,16},{18,... | collective-permute-start | bytes 2359304 | tf_op jit(solution)/shard_map/ppermute | solution.py:637
  317.0 19.5 %copy-start.59 = (f32[1,1536]{1,0:T(1,128)}, f32[1,1536]{1,0:T(1,128)S(1)}, u32[]{:S(2)}) copy-start(f32[1,1536]{1,0:T(1,128)S(1)} %get-tuple-element.213) | copy-start | bytes 18436
  317.0 23.5 %copy-start.8 = (bf16[1024,512]{1,0:T(8,128)(2,1)}, bf16[1024,512]{1,0:T(8,128)(2,1)S(1)}, u32[]{:S(2)}) copy-start(bf16[1024,512]{1,0:T(8,128)(2,1)S(1)} %get-tuple-element.185.branch_ref.refs_1_) | copy-start | bytes 3145732
  337.3 3.1 collective-permute-start.37
  353.3 389.5 %reduce-scatter.5.cloned.1.call-start = ((), (), s32[]{:S(2)}) async-start(), calls=%async_computation.3 | async-start | bytes 11943936 | tf_op jit(solution)/shard_map/reduce_scatter | solution.py:715
  377.6 29.7 %collective-permute-start.22 = (bf16[256,1536]{1,0:T(8,128)(2,1)S(1)}, bf16[256,1536]{1,0:T(8,128)(2,1)S(1)}, u32[]{:S(2)}, u32[]{:S(2)}) collective-permute-start(bf16[256,1536]{1,0:T(8,128)(2,1)S(1)} %copy-done.40), channel_id=1, source_target_pairs={{0,1},{3,2},{4,5},{7,6},{8,9},{11,10},{12,13},{15,14},{16,17},{19,... | collective-permute-start | bytes 2359304 | tf_op jit(solution)/shard_map/ppermute | solution.py:633
  391.2 33.0 %collective-permute-start.19 = (bf16[256,1536]{1,0:T(8,128)(2,1)S(1)}, bf16[256,1536]{1,0:T(8,128)(2,1)S(1)}, u32[]{:S(2)}, u32[]{:S(2)}) collective-permute-start(bf16[256,1536]{1,0:T(8,128)(2,1)S(1)} %copy-done.42), channel_id=1, source_target_pairs={{0,1},{3,2},{4,5},{7,6},{8,9},{11,10},{12,13},{15,14},{16,17},{19,... | collective-permute-start | bytes 2359304 | tf_op jit(solution)/shard_map/ppermute | solution.py:633
  392.5 48.5 %collective-permute-start.16 = (bf16[256,1536]{1,0:T(8,128)(2,1)S(1)}, bf16[256,1536]{1,0:T(8,128)(2,1)S(1)}, u32[]{:S(2)}, u32[]{:S(2)}) collective-permute-start(bf16[256,1536]{1,0:T(8,128)(2,1)S(1)} %copy-done.44), channel_id=1, source_target_pairs={{0,1},{3,2},{4,5},{7,6},{8,9},{11,10},{12,13},{15,14},{16,17},{19,... | collective-permute-start | bytes 2359304 | tf_op jit(solution)/shard_map/ppermute | solution.py:633
  393.9 64.0 %collective-permute-start.13 = (bf16[256,1536]{1,0:T(8,128)(2,1)S(1)}, bf16[256,1536]{1,0:T(8,128)(2,1)S(1)}, u32[]{:S(2)}, u32[]{:S(2)}) collective-permute-start(bf16[256,1536]{1,0:T(8,128)(2,1)S(1)} %copy-done.46), channel_id=1, source_target_pairs={{0,1},{3,2},{4,5},{7,6},{8,9},{11,10},{12,13},{15,14},{16,17},{19,... | collective-permute-start | bytes 2359304 | tf_op jit(solution)/shard_map/ppermute | solution.py:633
  407.5 51.3 %collective-permute-start.23 = (bf16[256,1536]{1,0:T(8,128)(2,1)S(1)}, bf16[256,1536]{1,0:T(8,128)(2,1)S(1)}, u32[]{:S(2)}, u32[]{:S(2)}) collective-permute-start(bf16[256,1536]{1,0:T(8,128)(2,1)S(1)} %add.169), channel_id=1, source_target_pairs={{1,2},{2,1},{5,6},{6,5},{9,10},{10,9},{13,14},{14,13},{17,18},{18,... | collective-permute-start | bytes 2359304 | tf_op jit(solution)/shard_map/ppermute | solution.py:635
  424.3 36.8 %collective-permute-start.20 = (bf16[256,1536]{1,0:T(8,128)(2,1)S(1)}, bf16[256,1536]{1,0:T(8,128)(2,1)S(1)}, u32[]{:S(2)}, u32[]{:S(2)}) collective-permute-start(bf16[256,1536]{1,0:T(8,128)(2,1)S(1)} %add.167), channel_id=1, source_target_pairs={{1,2},{2,1},{5,6},{6,5},{9,10},{10,9},{13,14},{14,13},{17,18},{18,... | collective-permute-start | bytes 2359304 | tf_op jit(solution)/shard_map/ppermute | solution.py:635
  441.2 22.6 %collective-permute-start.17 = (bf16[256,1536]{1,0:T(8,128)(2,1)S(1)}, bf16[256,1536]{1,0:T(8,128)(2,1)S(1)}, u32[]{:S(2)}, u32[]{:S(2)}) collective-permute-start(bf16[256,1536]{1,0:T(8,128)(2,1)S(1)} %add.165), channel_id=1, source_target_pairs={{1,2},{2,1},{5,6},{6,5},{9,10},{10,9},{13,14},{14,13},{17,18},{18,... | collective-permute-start | bytes 2359304 | tf_op jit(solution)/shard_map/ppermute | solution.py:635
  458.0 8.1 %collective-permute-start.14 = (bf16[256,1536]{1,0:T(8,128)(2,1)S(1)}, bf16[256,1536]{1,0:T(8,128)(2,1)S(1)}, u32[]{:S(2)}, u32[]{:S(2)}) collective-permute-start(bf16[256,1536]{1,0:T(8,128)(2,1)S(1)} %add.163), channel_id=1, source_target_pairs={{1,2},{2,1},{5,6},{6,5},{9,10},{10,9},{13,14},{14,13},{17,18},{18,... | collective-permute-start | bytes 2359304 | tf_op jit(solution)/shard_map/ppermute | solution.py:635
  459.8 23.6 %collective-permute-start.24 = (bf16[256,1536]{1,0:T(8,128)(2,1)}, bf16[256,1536]{1,0:T(8,128)(2,1)}, u32[]{:S(2)}, u32[]{:S(2)}) collective-permute-start(bf16[256,1536]{1,0:T(8,128)(2,1)} %add.170.t_ref), channel_id=1, source_target_pairs={{1,0},{2,3},{5,4},{6,7},{9,8},{10,11},{13,12},{14,15},{17,16},{18,... | collective-permute-start | bytes 2359304 | tf_op jit(solution)/shard_map/ppermute | solution.py:637
  462.2 21.2 %copy-start = (bf16[1024,1536]{1,0:T(8,128)(2,1)S(1)}, bf16[1024,1536]{1,0:T(8,128)(2,1)}, u32[]{:S(2)}) copy-start(bf16[1024,1536]{1,0:T(8,128)(2,1)} %x_ref.41) | copy-start | bytes 9437188
  462.2 38.1 %collective-permute-start.21 = (bf16[256,1536]{1,0:T(8,128)(2,1)}, bf16[256,1536]{1,0:T(8,128)(2,1)}, u32[]{:S(2)}, u32[]{:S(2)}) collective-permute-start(bf16[256,1536]{1,0:T(8,128)(2,1)} %add.168.t_ref), channel_id=1, source_target_pairs={{1,0},{2,3},{5,4},{6,7},{9,8},{10,11},{13,12},{14,15},{17,16},{18,... | collective-permute-start | bytes 2359304 | tf_op jit(solution)/shard_map/ppermute | solution.py:637
  464.8 52.3 %collective-permute-start.18 = (bf16[256,1536]{1,0:T(8,128)(2,1)}, bf16[256,1536]{1,0:T(8,128)(2,1)}, u32[]{:S(2)}, u32[]{:S(2)}) collective-permute-start(bf16[256,1536]{1,0:T(8,128)(2,1)} %add.166.t_ref), channel_id=1, source_target_pairs={{1,0},{2,3},{5,4},{6,7},{9,8},{10,11},{13,12},{14,15},{17,16},{18,... | collective-permute-start | bytes 2359304 | tf_op jit(solution)/shard_map/ppermute | solution.py:637
  467.2 66.8 %collective-permute-start.15 = (bf16[256,1536]{1,0:T(8,128)(2,1)}, bf16[256,1536]{1,0:T(8,128)(2,1)}, u32[]{:S(2)}, u32[]{:S(2)}) collective-permute-start(bf16[256,1536]{1,0:T(8,128)(2,1)} %add.164.t_ref), channel_id=1, source_target_pairs={{1,0},{2,3},{5,4},{6,7},{9,8},{10,11},{13,12},{14,15},{17,16},{18,... | collective-permute-start | bytes 2359304 | tf_op jit(solution)/shard_map/ppermute | solution.py:637
  544.3 36.7 %copy-start.52 = (bf16[256,1536]{1,0:T(8,128)(2,1)S(1)}, bf16[256,1536]{1,0:T(8,128)(2,1)}, u32[]{:S(2)}) copy-start(bf16[256,1536]{1,0:T(8,128)(2,1)} %copy-done.51) | copy-start | bytes 2359300
  544.3 19.8 %collective-permute-start.47 = (bf16[256,1536]{1,0:T(8,128)(2,1)}, bf16[256,1536]{1,0:T(8,128)(2,1)S(1)}, u32[]{:S(2)}, u32[]{:S(2)}) collective-permute-start(bf16[256,1536]{1,0:T(8,128)(2,1)} %copy-done.53), channel_id=1, source_target_pairs={{0,1},{3,2},{4,5},{7,6},{8,9},{11,10},{12,13},{15,14},{16,17},{19,... | collective-permute-start | bytes 2359304 | tf_op jit(solution)/shard_map/ppermute | solution.py:633
  546.0 35.0 %collective-permute-start.44 = (bf16[256,1536]{1,0:T(8,128)(2,1)}, bf16[256,1536]{1,0:T(8,128)(2,1)S(1)}, u32[]{:S(2)}, u32[]{:S(2)}) collective-permute-start(bf16[256,1536]{1,0:T(8,128)(2,1)} %copy-done.51), channel_id=1, source_target_pairs={{0,1},{3,2},{4,5},{7,6},{8,9},{11,10},{12,13},{15,14},{16,17},{19,... | collective-permute-start | bytes 2359304 | tf_op jit(solution)/shard_map/ppermute | solution.py:633
  547.3 50.5 %collective-permute-start.41 = (bf16[256,1536]{1,0:T(8,128)(2,1)}, bf16[256,1536]{1,0:T(8,128)(2,1)S(1)}, u32[]{:S(2)}, u32[]{:S(2)}) collective-permute-start(bf16[256,1536]{1,0:T(8,128)(2,1)} %copy-done.49), channel_id=1, source_target_pairs={{0,1},{3,2},{4,5},{7,6},{8,9},{11,10},{12,13},{15,14},{16,17},{19,... | collective-permute-start | bytes 2359304 | tf_op jit(solution)/shard_map/ppermute | solution.py:633
  548.7 66.0 %collective-permute-start.38 = (bf16[256,1536]{1,0:T(8,128)(2,1)}, bf16[256,1536]{1,0:T(8,128)(2,1)S(1)}, u32[]{:S(2)}, u32[]{:S(2)}) collective-permute-start(bf16[256,1536]{1,0:T(8,128)(2,1)} %copy-done.47), channel_id=1, source_target_pairs={{0,1},{3,2},{4,5},{7,6},{8,9},{11,10},{12,13},{15,14},{16,17},{19,... | collective-permute-start | bytes 2359304 | tf_op jit(solution)/shard_map/ppermute | solution.py:633
  550.0 2.0 collective-permute-start.50
  552.1 45.7 %copy-start.50 = (bf16[256,1536]{1,0:T(8,128)(2,1)S(1)}, bf16[256,1536]{1,0:T(8,128)(2,1)}, u32[]{:S(2)}) copy-start(bf16[256,1536]{1,0:T(8,128)(2,1)} %copy-done.49) | copy-start | bytes 2359300
  552.1 65.2 %collective-permute-start.51 = (bf16[544,256]{1,0:T(8,128)(2,1)S(1)}, bf16[544,256]{1,0:T(8,128)(2,1)S(1)}, u32[]{:S(2)}, u32[]{:S(2)}) collective-permute-start(bf16[544,256]{1,0:T(8,128)(2,1)S(1)} %add_convert_fusion.2), channel_id=1, source_target_pairs={{0,8},{4,12},{8,0},{12,4},{16,24},{20,28},{24,16},{28,20},{1,9},{5... | collective-permute-start | bytes 835592 | tf_op jit(solution)/shard_map/ppermute | solution.py:647
  566.3 48.4 %copy-start.48 = (bf16[256,1536]{1,0:T(8,128)(2,1)S(1)}, bf16[256,1536]{1,0:T(8,128)(2,1)}, u32[]{:S(2)}) copy-start(bf16[256,1536]{1,0:T(8,128)(2,1)} %copy-done.47) | copy-start | bytes 2359300
  566.3 96.5 %collective-permute-start.48 = (bf16[256,1536]{1,0:T(8,128)(2,1)}, bf16[256,1536]{1,0:T(8,128)(2,1)}, u32[]{:S(2)}, u32[]{:S(2)}) collective-permute-start(bf16[256,1536]{1,0:T(8,128)(2,1)} %add.186), channel_id=1, source_target_pairs={{1,2},{2,1},{5,6},{6,5},{9,10},{10,9},{13,14},{14,13},{17,18},{18,... | collective-permute-start | bytes 2359304 | tf_op jit(solution)/shard_map/ppermute | solution.py:635
  582.0 84.5 %collective-permute-start.45 = (bf16[256,1536]{1,0:T(8,128)(2,1)}, bf16[256,1536]{1,0:T(8,128)(2,1)}, u32[]{:S(2)}, u32[]{:S(2)}) collective-permute-start(bf16[256,1536]{1,0:T(8,128)(2,1)} %add.184), channel_id=1, source_target_pairs={{1,2},{2,1},{5,6},{6,5},{9,10},{10,9},{13,14},{14,13},{17,18},{18,... | collective-permute-start | bytes 2359304 | tf_op jit(solution)/shard_map/ppermute | solution.py:635
  598.9 71.4 %collective-permute-start.42 = (bf16[256,1536]{1,0:T(8,128)(2,1)}, bf16[256,1536]{1,0:T(8,128)(2,1)}, u32[]{:S(2)}, u32[]{:S(2)}) collective-permute-start(bf16[256,1536]{1,0:T(8,128)(2,1)} %add.182), channel_id=1, source_target_pairs={{1,2},{2,1},{5,6},{6,5},{9,10},{10,9},{13,14},{14,13},{17,18},{18,... | collective-permute-start | bytes 2359304 | tf_op jit(solution)/shard_map/ppermute | solution.py:635
  615.7 58.2 %collective-permute-start.39 = (bf16[256,1536]{1,0:T(8,128)(2,1)}, bf16[256,1536]{1,0:T(8,128)(2,1)}, u32[]{:S(2)}, u32[]{:S(2)}) collective-permute-start(bf16[256,1536]{1,0:T(8,128)(2,1)} %add.180), channel_id=1, source_target_pairs={{1,2},{2,1},{5,6},{6,5},{9,10},{10,9},{13,14},{14,13},{17,18},{18,... | collective-permute-start | bytes 2359304 | tf_op jit(solution)/shard_map/ppermute | solution.py:635
  617.4 61.3 %collective-permute-start.52 = (bf16[544,256]{1,0:T(8,128)(2,1)S(1)}, bf16[544,256]{1,0:T(8,128)(2,1)}, u32[]{:S(2)}, u32[]{:S(2)}) collective-permute-start(bf16[544,256]{1,0:T(8,128)(2,1)S(1)} %add_convert_fusion.1), channel_id=1, source_target_pairs={{0,16},{4,20},{8,24},{12,28},{16,0},{20,4},{24,8},{28,12},{1,17},{... | collective-permute-start | bytes 835592 | tf_op jit(solution)/shard_map/ppermute | solution.py:647
  665.2 22.7 %collective-permute-start.49 = (bf16[256,1536]{1,0:T(8,128)(2,1)}, bf16[256,1536]{1,0:T(8,128)(2,1)}, u32[]{:S(2)}, u32[]{:S(2)}) collective-permute-start(bf16[256,1536]{1,0:T(8,128)(2,1)} %add.187.t_ref), channel_id=1, source_target_pairs={{1,0},{2,3},{5,4},{6,7},{9,8},{10,11},{13,12},{14,15},{17,16},{18,... | collective-permute-start | bytes 2359304 | tf_op jit(solution)/shard_map/ppermute | solution.py:637
  669.0 35.8 %collective-permute-start.46 = (bf16[256,1536]{1,0:T(8,128)(2,1)}, bf16[256,1536]{1,0:T(8,128)(2,1)}, u32[]{:S(2)}, u32[]{:S(2)}) collective-permute-start(bf16[256,1536]{1,0:T(8,128)(2,1)} %add.185.t_ref), channel_id=1, source_target_pairs={{1,0},{2,3},{5,4},{6,7},{9,8},{10,11},{13,12},{14,15},{17,16},{18,... | collective-permute-start | bytes 2359304 | tf_op jit(solution)/shard_map/ppermute | solution.py:637
  672.7 48.9 %collective-permute-start.43 = (bf16[256,1536]{1,0:T(8,128)(2,1)}, bf16[256,1536]{1,0:T(8,128)(2,1)}, u32[]{:S(2)}, u32[]{:S(2)}) collective-permute-start(bf16[256,1536]{1,0:T(8,128)(2,1)} %add.183.t_ref), channel_id=1, source_target_pairs={{1,0},{2,3},{5,4},{6,7},{9,8},{10,11},{13,12},{14,15},{17,16},{18,... | collective-permute-start | bytes 2359304 | tf_op jit(solution)/shard_map/ppermute | solution.py:637
  676.4 60.0 %collective-permute-start.40 = (bf16[256,1536]{1,0:T(8,128)(2,1)}, bf16[256,1536]{1,0:T(8,128)(2,1)}, u32[]{:S(2)}, u32[]{:S(2)}) collective-permute-start(bf16[256,1536]{1,0:T(8,128)(2,1)} %add.181.t_ref), channel_id=1, source_target_pairs={{1,0},{2,3},{5,4},{6,7},{9,8},{10,11},{13,12},{14,15},{17,16},{18,... | collective-permute-start | bytes 2359304 | tf_op jit(solution)/shard_map/ppermute | solution.py:637
  (57 other events, 366.4 us)
Sparse Core Ops, SparseCore 0:
  353.4 63.5 reduce-scatter.2
  420.9 82.1 reduce-scatter.4
